TPU v7x, 512 devices: a whole 4x4x16 slice. The times are simulated.
512 devices in a mesh: dp: 16 (over z_hi, y), mp: 32 (over z_lo, x, core).
Axes of the slice: x: 4, y: 4, z: 16 (z_hi: 4, z_lo: 4; z = z_hi * 4 + z_lo), core: 2. Of those that a mesh axis runs over, the one named last changes fastest.
Arguments:
- teacher_hidden: bfloat16 [224, 26624], P('dp', 'mp'), may hold values from -6 to 6
- teacher_down: bfloat16 [26624, 16384], P('mp', 'dp'), may hold values from -0.0390625 to 0.0390625
- scale_index: int32 [416], P('mp'), may hold values from 0 to 6
- distill_proj: bfloat16 [16384, 8192], P('dp', 'mp'), may hold values from -0.046875 to 0.046875
- assignment: int32 [224], replicated, may hold values from 0 to 223, each once
- student_input: bfloat16 [224, 8192], P('dp', 'mp'), may hold values from -6 to 6
- w_gate: bfloat16 [8192, 14336], P('mp', 'dp'), may hold values from -0.0625 to 0.0625
- w_up: bfloat16 [8192, 14336], P('mp', 'dp'), may hold values from -0.0625 to 0.0625
- w_down: bfloat16 [14336, 8192], P('dp', 'mp'), may hold values from -0.046875 to 0.046875
Outputs:
- grad_gate: bfloat16 [8192, 14336], P('mp', 'dp')
- grad_up: bfloat16 [8192, 14336], P('mp', 'dp')
- grad_down: bfloat16 [14336, 8192], P('dp', 'mp')
- input_grad: bfloat16 [224, 8192], P('dp', 'mp')
All inputs are finite; a program needn't handle non-finite values. Where the computation divides by a largest or mean magnitude, that divisor is 1e-20 or more.
Results may differ from a plain program's by a relative error of at most 0.008.
Values may be sent and summed in bfloat16 or wider, within the bound.
A program may use at most 64 MiB of HBM per device.

v0:
```python
import jax
import jax.numpy as jnp
from jax import lax
from jax.sharding import PartitionSpec as P

target_range = 4.0


def contract_rows(left, right):
    return lax.dot_general(
        left, right, (((0,), (0,)), ((), ())), preferred_element_type=jnp.float32
    )


def contract_cols(left, right):
    return lax.dot_general(
        left, right, (((1,), (1,)), ((), ())), preferred_element_type=jnp.float32
    )


def body(
    teacher_hidden,
    teacher_down,
    scale_index,
    distill_proj,
    assignment,
    student_input,
    w_gate,
    w_up,
    w_down,
):
    group_width = teacher_hidden.shape[1] // scale_index.shape[0]
    scales = jnp.repeat(jnp.exp2(scale_index.astype(jnp.float32) - 3.0), group_width)
    scaled = (
        lax.all_gather(teacher_hidden, "dp", axis=0, tiled=True).astype(jnp.float32) * scales
    ).astype(jnp.bfloat16)
    partial_out = jnp.dot(scaled, teacher_down, preferred_element_type=jnp.float32)
    teacher_out = lax.psum(partial_out, "mp").astype(jnp.bfloat16)
    local_max = jnp.max(jnp.abs(teacher_out.astype(jnp.float32)))
    amax = lax.pmax(local_max, ("dp", "mp"))
    picked = jnp.take(teacher_out, assignment, axis=0)
    target = lax.psum_scatter(
        jnp.dot(picked, distill_proj, preferred_element_type=jnp.float32),
        "dp",
        scatter_dimension=0,
        tiled=True,
    ) * (target_range / amax)
    inputs_all = lax.all_gather(student_input, "dp", axis=0, tiled=True)
    gate_part = jnp.dot(inputs_all, w_gate, preferred_element_type=jnp.float32)
    up_part = jnp.dot(inputs_all, w_up, preferred_element_type=jnp.float32)
    gate_all, up_all = lax.psum((gate_part, up_part), "mp")
    hidden_all = (jax.nn.silu(gate_all) * up_all).astype(jnp.bfloat16)
    share = gate_all.shape[0] // lax.axis_size("mp")
    offset = lax.axis_index("mp") * share
    gate = lax.dynamic_slice_in_dim(gate_all, offset, share, 0)
    up = lax.dynamic_slice_in_dim(up_all, offset, share, 0)
    rows = hidden_all
    student_out = lax.psum_scatter(
        jnp.dot(rows, w_down, preferred_element_type=jnp.float32),
        "dp",
        scatter_dimension=0,
        tiled=True,
    )
    out_grad = ((student_out - target) * 0.5).astype(jnp.bfloat16)
    grad_all = lax.all_gather(out_grad, "dp", axis=0, tiled=True)
    grad_down = contract_rows(hidden_all, grad_all).astype(jnp.bfloat16)
    rows = grad_all
    hidden_grad = lax.psum_scatter(
        contract_cols(rows, w_down), "mp", scatter_dimension=0, tiled=True
    )
    sig = jax.nn.sigmoid(gate)
    gate_grad = (hidden_grad * up * sig * (1.0 + gate * (1.0 - sig))).astype(jnp.bfloat16)
    up_grad = (hidden_grad * gate * sig).astype(jnp.bfloat16)
    gate_grad_all, up_grad_all = (
        lax.all_gather(gate_grad, "mp", axis=0, tiled=True),
        lax.all_gather(up_grad, "mp", axis=0, tiled=True),
    )
    grad_gate = contract_rows(inputs_all, gate_grad_all).astype(jnp.bfloat16)
    grad_up = contract_rows(inputs_all, up_grad_all).astype(jnp.bfloat16)
    input_grad = lax.psum_scatter(
        contract_cols(gate_grad_all, w_gate) + contract_cols(up_grad_all, w_up),
        "dp",
        scatter_dimension=0,
        tiled=True,
    ).astype(jnp.bfloat16)
    return (grad_gate, grad_up, grad_down, input_grad)


def solution(mesh):
    placed = (
        P("dp", "mp"),
        P("mp", "dp"),
        P("mp"),
        P("dp", "mp"),
        P(),
        P("dp", "mp"),
        P("mp", "dp"),
        P("mp", "dp"),
        P("dp", "mp"),
    )
    return jax.shard_map(
        body,
        mesh=mesh,
        in_specs=placed,
        out_specs=(P("mp", "dp"), P("mp", "dp"), P("dp", "mp"), P("dp", "mp")),
        check_vma=False,
    )
```

profile of v0, /device:TPU:1, one launch (start us, length us, event | category | flops | bytes accessed | tf_op | source)
XLA Modules:
  0.0 1004.5 jit_solution(5843765281810149765)
XLA Ops:
  7.2 0.0 copy-start
  7.2 0.0 copy-start.5
  7.2 0.0 all-reduce.15.cloned.1.call-start
  7.2 53.1 %all-gather = bf16[16,14,256]{2,1,0:T(8,128)(2,1)S(1)} all-gather(bf16[1,14,256]{2,1,0:T(8,128)(2,1)} %bitcast.42), channel_id=1, replica_groups=mesh['dp'=16,'mp'=32] {'dp'}, dimensions={0}, use_global_device_ids=true | all-gather | bytes 121856 | tf_op jit(solution)/shard_map/all_gather | solution.py:48
  60.4 0.0 copy-start.1
  60.4 2.2 fusion.20
  62.6 1.2 fusion.19
  63.8 0.0 all-reduce.15.cloned.1.call-update
  63.8 0.0 copy-done.1
  63.8 0.0 all-reduce.13.cloned.1.call-start
  63.9 0.0 copy-done.9
  63.9 0.1 broadcast_in_dim.16
  64.0 0.1 mul.52
  64.1 49.0 %all-gather.1 = bf16[16,14,832]{2,1,0:T(8,128)(2,1)S(1)} all-gather(bf16[1,14,832]{2,1,0:T(8,128)(2,1)S(1)} %bitcast.41), channel_id=1, replica_groups=mesh['dp'=16,'mp'=32] {'dp'}, dimensions={0}, use_global_device_ids=true | all-gather | bytes 396032 | tf_op jit(solution)/shard_map/all_gather | solution.py:35
  113.0 0.2 reshape.33
  113.2 0.0 copy-start.8
  113.2 0.6 fusion.8
  113.8 0.0 copy-done.8
  113.9 149.4 %all-reduce.16 = bf16[224,1024]{1,0:T(8,128)(2,1)S(1)} all-reduce(f32[224,1024]{1,0:T(8,128)S(1)} %fusion.8), channel_id=1, replica_groups=mesh['dp'=16,'mp'=32] {'mp'}, use_global_device_ids=true, to_apply=%region_3.4 | all-reduce | flops 229376 | bytes 1376256 | tf_op jit(solution)/shard_map/psum | solution.py:38
  263.3 1.1 gather_fusion
  264.4 0.0 copy-start.4
  264.4 2.1 fusion.5
  266.6 81.0 %all-reduce.15.cloned.1.call-done = (f32[224,896]{1,0:T(8,128)}, f32[224,896]{1,0:T(8,128)}) async-done(((f32[224,896]{1,0:T(8,128)}, f32[224,896]{1,0:T(8,128)}), (f32[224,896]{1,0:T(8,128)}, f32[224,896]{1,0:T(8,128)})) %all-reduce.15.cloned.1.call-update) | async-done | bytes 1605648 | tf_op jit(solution)/shard_map/psum | solution.py:51
  347.5 1.6 multiply_convert_fusion.1
  349.2 0.3 fusion.21
  349.5 52.4 %fusion.18 = (f32[16,256]{1,0:T(8,128)S(1)}, f32[16,256]{1,0:T(8,128)S(1)}) fusion(f32[224,256]{1,0:T(8,128)S(1)} %copy-done.6, f32[224,256]{1,0:T(8,128)S(1)} %fusion.21), kind=kCustom, calls=%all-reduce-scatter.3 | all-reduce-scatter fusion | flops 131073 | bytes 493568
  401.9 1.3 collective-permute-start.2
  403.2 1.3 collective-permute-start
  404.5 5.3 collective-permute-start.1
  409.8 1.9 collective-permute-start.3
  411.7 0.7 abs_reduce_fusion
  412.4 114.7 %pmax.7 = f32[]{:T(128)} all-reduce(f32[]{:T(128)} %abs_reduce_fusion), channel_id=1, replica_groups=mesh['dp'=16,'mp'=32] {'dp','mp'}, use_global_device_ids=true, to_apply=%region_6.7 | all-reduce | flops 1 | bytes 8 | tf_op jit(solution)/shard_map/pmax | solution.py:40
  527.1 1.3 dynamic-slice.10
  529.7 0.0 collective-permute-done.3
  529.7 0.0 collective-permute-done.2
  529.7 0.3 concatenate.1
  530.0 0.0 collective-permute-done.1
  530.0 0.0 collective-permute-done
  530.0 0.3 concatenate
  530.3 43.0 %all-gather.2 = bf16[16,14,256]{2,1,0:T(8,128)(2,1)S(1)} all-gather(bf16[1,14,256]{2,1,0:T(8,128)(2,1)S(1)} %fusion.16), channel_id=1, replica_groups=mesh['dp'=16,'mp'=32] {'dp'}, dimensions={0}, use_global_device_ids=true | all-gather | bytes 121856 | tf_op jit(solution)/shard_map/all_gather | solution.py:65
  573.3 1.2 fusion.22
  574.6 0.0 all-reduce.13.cloned.1.call-update
  574.6 1.3 dynamic-slice.4
  576.5 1.1 convolution_convert_fusion
  577.7 276.0 %all-reduce.13.cloned.1.call-done = f32[224,896]{1,0:T(8,128)} async-done(((f32[224,896]{1,0:T(8,128)}), f32[224,896]{1,0:T(8,128)}) %all-reduce.13.cloned.1.call-update) | async-done | bytes 802832
  853.7 0.9 fusion.14
  854.6 40.9 %all-gather.4 = bf16[32,7,896]{2,1,0:T(8,128)(2,1)S(1)} all-gather(bf16[1,7,896]{2,1,0:T(8,128)(2,1)S(1)} %get-tuple-element.22), channel_id=1, replica_groups=mesh['dp'=16,'mp'=32] {'mp'}, dimensions={0}, use_global_device_ids=true | all-gather | bytes 413952 | tf_op jit(solution)/shard_map/all_gather | solution.py:76
  895.4 0.1 reshape.32
  895.6 0.0 copy-start.3
  895.6 0.3 fusion.4
  896.0 43.4 %all-gather.3 = bf16[32,7,896]{2,1,0:T(8,128)(2,1)} all-gather(bf16[1,7,896]{2,1,0:T(8,128)(2,1)S(1)} %get-tuple-element.23), channel_id=1, replica_groups=mesh['dp'=16,'mp'=32] {'mp'}, dimensions={0}, use_global_device_ids=true | all-gather | bytes 413952 | tf_op jit(solution)/shard_map/all_gather | solution.py:75
  939.3 1.2 reshape.30
  940.5 1.3 fusion.23
  941.9 1.0 convolution_add_fusion
  942.9 48.9 %fusion.2 = f32[16,256]{1,0:T(8,128)S(1)} fusion(f32[224,256]{1,0:T(8,128)} %convolution_add_fusion), kind=kCustom, calls=%all-reduce-scatter.2 | all-reduce-scatter fusion | flops 65537 | bytes 247808
  991.9 1.3 collective-permute-start.4
  993.2 1.3 collective-permute-start.5
  994.4 0.3 fusion.3
  994.8 1.0 copy.18
  995.8 1.0 copy.17
  996.8 0.0 collective-permute-done.5
  996.8 0.0 collective-permute-done.4
  996.8 0.3 concatenate.2
  997.0 0.6 dynamic-slice_convert_fusion
  (22 shorter events, 0.2 us)
Async XLA Ops:
  7.2 106.0 %copy-start = (bf16[832,1024]{1,0:T(8,128)(2,1)S(1)}, bf16[832,1024]{1,0:T(8,128)(2,1)}, u32[]{:S(2)}) copy-start(bf16[832,1024]{1,0:T(8,128)(2,1)} %param.10) | copy-start | bytes 5111812
  7.2 55.4 %copy-start.5 = (bf16[256,896]{1,0:T(8,128)(2,1)S(1)}, bf16[256,896]{1,0:T(8,128)(2,1)}, u32[]{:S(2)}) copy-start(bf16[256,896]{1,0:T(8,128)(2,1)} %param.15) | copy-start | bytes 1376260
  7.2 340.3 %all-reduce.15.cloned.1.call-start = ((), (), s32[]{:S(2)}) async-start(), calls=%async_computation.1 | async-start | bytes 3211264 | tf_op jit(solution)/shard_map/psum | solution.py:51
  60.4 3.4 copy-start.1
  62.6 1.3 copy-start.9
  62.6 1.4 copy-start.7
  63.8 789.8 %all-reduce.13.cloned.1.call-start = ((), (), s32[]{:S(2)}) async-start(), calls=%async_computation | async-start | bytes 1605632
  113.2 0.7 copy-start.8
  264.4 84.7 %copy-start.4 = (bf16[896,256]{1,0:T(8,128)(2,1)S(1)}, bf16[896,256]{1,0:T(8,128)(2,1)}, u32[]{:S(2)}) copy-start(bf16[896,256]{1,0:T(8,128)(2,1)} %param.17) | copy-start | bytes 1376260
  266.6 82.9 %copy-start.6 = (f32[224,256]{1,0:T(8,128)S(1)}, f32[224,256]{1,0:T(8,128)}, u32[]{:S(2)}) copy-start(f32[224,256]{1,0:T(8,128)} %fusion.5) | copy-start | bytes 688132
  401.9 127.8 %collective-permute-start.2 = (f32[16,256]{1,0:T(8,128)S(1)}, f32[16,256]{1,0:T(8,128)S(1)}, u32[]{:S(2)}, u32[]{:S(2)}) collective-permute-start(f32[16,256]{1,0:T(8,128)S(1)} %get-tuple-element.20), channel_id=1, source_target_pairs={{0,32},{32,64},{64,96},{96,128},{128,160},{160,192},{192,224},{224... | collective-permute-start | bytes 49160
  403.2 126.8 %collective-permute-start = (f32[16,256]{1,0:T(8,128)S(1)}, f32[16,256]{1,0:T(8,128)S(1)}, u32[]{:S(2)}, u32[]{:S(2)}) collective-permute-start(f32[16,256]{1,0:T(8,128)S(1)} %get-tuple-element.21), channel_id=1, source_target_pairs={{0,32},{32,64},{64,96},{96,128},{128,160},{160,192},{192,224},{224... | collective-permute-start | bytes 49160
  404.5 125.5 %collective-permute-start.1 = (f32[14,256]{1,0:T(8,128)S(1)}, f32[14,256]{1,0:T(8,128)S(1)}, u32[]{:S(2)}, u32[]{:S(2)}) collective-permute-start(f32[14,256]{1,0:T(8,128)S(1)} %slice.2), channel_id=1, source_target_pairs={{0,64},{32,96},{64,128},{96,160},{128,192},{160,224},{192,256},{22... | collective-permute-start | bytes 43016
  409.8 119.9 %collective-permute-start.3 = (f32[14,256]{1,0:T(8,128)S(1)}, f32[14,256]{1,0:T(8,128)S(1)}, u32[]{:S(2)}, u32[]{:S(2)}) collective-permute-start(f32[14,256]{1,0:T(8,128)S(1)} %slice.3), channel_id=1, source_target_pairs={{0,64},{32,96},{64,128},{96,160},{128,192},{160,224},{192,256},{22... | collective-permute-start | bytes 43016
  574.6 321.0 %copy-start.2 = (bf16[224,256]{1,0:T(8,128)(2,1)S(1)}, bf16[224,256]{1,0:T(8,128)(2,1)}, u32[]{:S(2)}) copy-start(bf16[224,256]{1,0:T(8,128)(2,1)} %copy-done.1) | copy-start | bytes 344068
  895.6 46.3 %copy-start.3 = (bf16[256,896]{1,0:T(8,128)(2,1)S(1)}, bf16[256,896]{1,0:T(8,128)(2,1)}, u32[]{:S(2)}) copy-start(bf16[256,896]{1,0:T(8,128)(2,1)} %param.16) | copy-start | bytes 1376260
  991.9 4.9 collective-permute-start.4
  993.2 3.6 collective-permute-start.5
Sparse Core Ops, SparseCore 0:
  63.9 283.5 all-reduce.14
  574.7 278.9 all-reduce.12
where the time goes:
time: 1020 us; the launch traced here: 1000 us
  blocking collectives  595 us (58%)
  waiting for transfers between devices  357 us (35%)
  between operations  16.4 us (2%)
  starting transfers between devices  12.5 us (1%)
  matrix products  11.8 us (1%)
    unnamed x9, waiting for transfers between devices  276 us
    psum x1, blocking collectives, body(): teacher_out = lax.psum(partial_out, 'mp').astype(jnp.bfloat16)  149 us
    pmax x1, blocking collectives, body(): amax = lax.pmax(local_max, ('dp', 'mp'))  115 us
    unnamed x2, blocking collectives  101 us
    psum x1, waiting for transfers between devices, body(): gate_all, up_all = lax.psum((gate_part, up_part), 'mp')  81 us
    all_gather x1, blocking collectives, body(): inputs_all = lax.all_gather(student_input, 'dp', axis=0, tiled=True)  53.1 us
    all_gather x1, blocking collectives, body(): lax.all_gather(teacher_hidden, 'dp', axis=0, tiled=True).astype(jnp.float32)  49 us
    all_gather x1, blocking collectives, body(): lax.all_gather(gate_grad, 'mp', axis=0, tiled=True)  43.4 us
  transfers between devices with their start and end apart: 8, of which 2 were waited for; matrix products, arithmetic and copies ran while one was open for 1% of the time, Pallas kernels for 0%

commit v1 on v0

v1 whole, which is shorter than its diff:
```python
import functools

import jax
import jax.numpy as jnp
from jax import lax
from jax.experimental import pallas as pl
from jax.experimental.pallas import tpu as pltpu
from jax.sharding import PartitionSpec as P

MESH = pl.DeviceIdType.MESH
BF, F32 = jnp.bfloat16, jnp.float32
ROWS = 16
KS = (1, 3, 2)

RECV = {}
N_RECV = 0
for _name, _n in (
    ("Sz", 4), ("Sy", 16), ("Tz", 4), ("Ty", 16), ("Sc", 2), ("Tc", 1), ("Sx", 4), ("Tx", 4), ("Szl", 4), ("Tzl", 4),
    ("Hzl", 4), ("ABzl", 4), ("Hx", 4), ("Hc", 4), ("ABx", 4), ("ABc", 4), ("Tax", 4), ("Tac", 4),
    ("Mz", 4), ("My", 4), ("Mx", 4), ("Mc", 1), ("TPy", 4), ("SPy", 4), ("Oz", 4), ("Oy", 4),
    ("Gc", 1), ("Gx", 4), ("Gzl", 4), ("Gax", 4), ("Gac", 4), ("Iy", 4), ("Iz", 4),
):
    RECV[_name] = N_RECV
    N_RECV += _n
N_SEND = 150


def dot(a, b):
    return jnp.dot(a, b, preferred_element_type=F32)


def dot_nt(a, b):
    return lax.dot_general(a, b, (((1,), (1,)), ((), ())), preferred_element_type=F32)


def dot_tn(a, b):
    return lax.dot_general(a, b, (((0,), (0,)), ((), ())), preferred_element_type=F32)


def kernel(
    th, xin, perm, td_h, dp_h, wg_h, wu_h, wd_h,
    gg_o, gu_o, gd_o, ig_o,
    td, dpj, wg, wu, wd, TG, XG, XT,
    SCs, SCr, SOWN, SXs, SXr, SZf, SZs, SZr, HZ, ABZ, HID, AB,
    TCs, TCr, TOWN, TXs, TXr, TZ, TO, AM0, AMz, AMy, AMx, AMc,
    TPf, TPr, SPf, SPr, OZ, OG,
    GCs, GCr, GOWN, GXs, GXr, GZ, HG, GG, UG, IPf, IPs, IPr, IZf, IZs, IZr,
    send_sem, recv_sem, load_sem,
):
    d, m = lax.axis_index("dp"), lax.axis_index("mp")
    zh, y, zl, x, c = d // 4, d % 4, m // 8, (m // 2) % 4, m % 2
    oc = 1 - c

    def turn(v, k):
        return lax.rem(v + k, 4)

    def at(zh=zh, y=y, zl=zl, x=x, c=c):
        return (zh * 4 + y, zl * 8 + x * 2 + c)

    core = at(c=oc)
    x_dev = lambda v: at(x=v)
    y_dev = lambda v: at(y=v)
    zl_dev = lambda v: at(zl=v)
    zh_dev = lambda v: at(zh=v)

    sent = []

    def send(src, dst, dev, name, slot):
        copy = pltpu.make_async_remote_copy(
            src, dst, send_sem.at[len(sent)], recv_sem.at[RECV[name] + slot], device_id=dev, device_id_type=MESH
        )
        copy.start()
        sent.append(copy)

    def arrive(dst, name, slot):
        pltpu.make_async_remote_copy(
            dst, dst, send_sem.at[0], recv_sem.at[RECV[name] + slot], device_id=core, device_id_type=MESH
        ).wait_recv()

    barrier = pltpu.get_barrier_semaphore()
    partners = [core]
    for k in KS:
        partners += [x_dev(turn(x, k)), y_dev(turn(y, k)), zl_dev(turn(zl, k)), zh_dev(turn(zh, k))]
    for p in partners:
        pl.semaphore_signal(barrier, inc=1, device_id=p, device_id_type=MESH)
    loads = [
        pltpu.make_async_copy(a, b, load_sem.at[i])
        for i, (a, b) in enumerate(((wg_h, wg), (wu_h, wu), (td_h, td), (dp_h, dpj), (wd_h, wd)))
    ]
    for load in loads:
        load.start()
    XG[zh, y] = xin[...]
    TG[zh, y] = th[...]
    pl.semaphore_wait(barrier, len(partners))

    for buf, nz, ny in ((XG, "Sz", "Sy"), (TG, "Tz", "Ty")):
        own = buf.at[zh, y]
        for k in KS:
            send(own, own, zh_dev(turn(zh, k)), nz, zh)
        for k in KS:
            send(own, own, y_dev(turn(y, k)), ny, zh * 4 + y)
    for buf, nz, ny in ((XG, "Sz", "Sy"), (TG, "Tz", "Ty")):
        for k in KS:
            z = turn(zh, k)
            arrive(buf.at[z, y], nz, z)
            for j in KS:
                send(buf.at[z, y], buf.at[z, y], y_dev(turn(y, j)), ny, z * 4 + y)

    for j in KS:
        for z in range(4):
            arrive(XG.at[z, turn(y, j)], "Sy", z * 4 + turn(y, j))
    loads[0].wait()
    loads[1].wait()
    half = XG[pl.ds(2 * oc, 2)].reshape(128, -1)
    for a, w in enumerate((wg, wu)):
        SCs[a] = dot(half, w[...]).reshape(SCs.shape[1:])
        send(SCs.at[a], SCr.at[a], core, "Sc", a)
    half = XG[pl.ds(2 * c, 2)].reshape(128, -1)
    for a, w in enumerate((wg, wu)):
        SOWN[a] = dot(half, w[...]).reshape(SOWN.shape[1:])

    for j in KS:
        for z in range(4):
            arrive(TG.at[z, turn(y, j)], "Ty", z * 4 + turn(y, j))
    loads[2].wait()
    everything = TG[...].reshape(16 * ROWS, -1)
    picked = dot(perm[pl.ds(oc, 1)].reshape(128, -1), everything).astype(BF)
    TCs[...] = dot(picked, td[...]).reshape(TCs.shape)
    send(TCs, TCr, core, "Tc", 0)
    picked = dot(perm[pl.ds(c, 1)].reshape(128, -1), everything).astype(BF)
    TOWN[...] = dot(picked, td[...]).reshape(TOWN.shape)

    for a in range(2):
        arrive(SCr.at[a], "Sc", a)
    for k in KS:
        v = turn(x, k)
        for a in range(2):
            SXs[v, a] = (SOWN[a, v] + SCr[a, v]).astype(BF)
        send(SXs.at[v], SXr.at[x], x_dev(v), "Sx", x)
    arrive(TCr, "Tc", 0)
    for k in KS:
        v = turn(x, k)
        TXs[v] = (TOWN[v] + TCr[v]).astype(BF)
        send(TXs.at[v], TXr.at[x], x_dev(v), "Tx", x)
    XT[...] = XG[...].reshape(16 * ROWS, -1).T

    fs = SOWN.shape[-1]
    shift = fs - 512
    for k in KS:
        arrive(SXr.at[turn(x, k)], "Sx", turn(x, k))
    for a in range(2):
        total = SOWN[a, x] + SCr[a, x]
        for k in KS:
            total = total + SXr[turn(x, k), a].astype(F32)
        for w in range(4):
            r, h = w % 2, w // 2
            part = total[r * 16 : r * 16 + 16, h * shift : h * shift + 512]
            SZf[w, a] = part
            SZs[w, a] = part.astype(BF)
    for k in KS:
        v = turn(zl, k)
        send(SZs.at[v], SZr.at[zl], zl_dev(v), "Szl", zl)
    for k in KS:
        arrive(TXr.at[turn(x, k)], "Tx", turn(x, k))
    total = TOWN[x] + TCr[x]
    for k in KS:
        total = total + TXr[turn(x, k)].astype(F32)
    TZ[zl] = total.astype(BF)
    for k in KS:
        send(TZ.at[zl], TZ.at[zl], zl_dev(turn(zl, k)), "Tzl", zl)

    for k in KS:
        arrive(SZr.at[turn(zl, k)], "Szl", turn(zl, k))
    pre = []
    for a in range(2):
        total = SZf[zl, a]
        for k in KS:
            total = total + SZr[turn(zl, k), a].astype(F32)
        pre.append(total)
    gate, up = pre
    sig = jax.nn.sigmoid(gate)
    HZ[zl] = (gate * sig * up).astype(BF)
    for k in KS:
        send(HZ.at[zl], HZ.at[zl], zl_dev(turn(zl, k)), "Hzl", zl)
    ABZ[zl, 0] = (up * sig * (1.0 + gate * (1.0 - sig))).astype(BF)
    ABZ[zl, 1] = (gate * sig).astype(BF)
    for k in KS:
        send(ABZ.at[zl], ABZ.at[zl], zl_dev(turn(zl, k)), "ABzl", zl)

    for k in KS:
        arrive(TZ.at[turn(zl, k)], "Tzl", turn(zl, k))
    total = TZ[0].astype(F32)
    for w in range(1, 4):
        total = total + TZ[w].astype(F32)
    teacher = total.astype(BF)
    TO[c, x] = teacher
    for k in KS:
        send(TO.at[c, x], TO.at[c, x], x_dev(turn(x, k)), "Tax", x)
    send(TO.at[c, x], TO.at[c, x], core, "Tac", x)
    AM0[...] = jnp.full(AM0.shape, jnp.max(jnp.abs(teacher.astype(F32))), F32)
    for k in KS:
        send(AM0, AMz.at[zh], zh_dev(turn(zh, k)), "Mz", zh)

    for k in KS:
        arrive(HZ.at[turn(zl, k)], "Hzl", turn(zl, k))
    for r in range(2):
        HID[c, x, r, :, 0:512] = HZ[r]
        HID[c, x, r, :, 512:fs] = HZ[2 + r][:, 512 - shift :]
    for k in KS:
        send(HID.at[c, x], HID.at[c, x], x_dev(turn(x, k)), "Hx", x)
    send(HID.at[c, x], HID.at[c, x], core, "Hc", x)

    for k in KS:
        v = turn(x, k)
        arrive(TO.at[c, v], "Tax", v)
        send(TO.at[c, v], TO.at[c, v], core, "Tac", v)
    for k in KS:
        v = turn(x, k)
        arrive(HID.at[c, v], "Hx", v)
        send(HID.at[c, v], HID.at[c, v], core, "Hc", v)
    biggest = AM0[...]
    for k in KS:
        arrive(AMz.at[turn(zh, k)], "Mz", turn(zh, k))
        biggest = jnp.maximum(biggest, AMz[turn(zh, k)])
    AMy[y] = biggest
    for k in KS:
        send(AMy.at[y], AMy.at[y], y_dev(turn(y, k)), "My", y)

    loads[3].wait()
    for w in range(4):
        arrive(TO.at[oc, w], "Tac", w)
    part = dot(TO[...].reshape(16 * ROWS, -1), dpj[...]).reshape(TPf.shape)
    TPf[...] = part
    for k in KS:
        v = turn(y, k)
        send(TPf.at[:, v], TPr.at[y], y_dev(v), "TPy", y)
    loads[4].wait()
    for w in range(4):
        arrive(HID.at[oc, w], "Hc", w)
    part = dot(HID[...].reshape(16 * ROWS, -1), wd[...]).reshape(SPf.shape)
    SPf[...] = part
    for k in KS:
        v = turn(y, k)
        send(SPf.at[:, v], SPr.at[y], y_dev(v), "SPy", y)

    for k in KS:
        arrive(AMy.at[turn(y, k)], "My", turn(y, k))
    AMx[x] = jnp.maximum(jnp.maximum(AMy[0], AMy[1]), jnp.maximum(AMy[2], AMy[3]))
    for k in KS:
        send(AMx.at[x], AMx.at[x], x_dev(turn(x, k)), "Mx", x)
    for k in KS:
        arrive(ABZ.at[turn(zl, k)], "ABzl", turn(zl, k))
    for a in range(2):
        for r in range(2):
            AB[c, x, a, r, :, 0:512] = ABZ[r, a]
            AB[c, x, a, r, :, 512:fs] = ABZ[2 + r, a][:, 512 - shift :]
    for k in KS:
        arrive(AMx.at[turn(x, k)], "Mx", turn(x, k))
    biggest = jnp.maximum(jnp.maximum(AMx[0], AMx[1]), jnp.maximum(AMx[2], AMx[3]))
    AM0c = AMc.at[0]
    AM0c[...] = biggest
    send(AMc.at[0], AMc.at[1], core, "Mc", 0)
    for k in KS:
        send(AB.at[c, x], AB.at[c, x], x_dev(turn(x, k)), "ABx", x)
    send(AB.at[c, x], AB.at[c, x], core, "ABc", x)

    for k in KS:
        arrive(TPr.at[turn(y, k)], "TPy", turn(y, k))
        arrive(SPr.at[turn(y, k)], "SPy", turn(y, k))
    arrive(AMc.at[1], "Mc", 0)
    scale = (4.0 / jnp.maximum(biggest, AMc[1]))[0:1, 0:1]
    for z in range(4):
        target, student = TPf[z, y], SPf[z, y]
        for k in KS:
            target = target + TPr[turn(y, k), z]
            student = student + SPr[turn(y, k), z]
        OZ[zh, z] = ((student - target * scale) * 0.5).astype(BF)
    for k in KS:
        send(OZ.at[zh], OZ.at[zh], zh_dev(turn(zh, k)), "Oz", zh)
    for k in KS:
        v = turn(x, k)
        arrive(AB.at[c, v], "ABx", v)
        send(AB.at[c, v], AB.at[c, v], core, "ABc", v)
    for k in KS:
        arrive(OZ.at[turn(zh, k)], "Oz", turn(zh, k))
    for z in range(4):
        total = OZ[0, z].astype(F32)
        for w in range(1, 4):
            total = total + OZ[w, z].astype(F32)
        OG[z, y] = total.astype(BF)
    for k in KS:
        send(OG.at[:, y], OG.at[:, y], y_dev(turn(y, k)), "Oy", y)
    for k in KS:
        arrive(OG.at[:, turn(y, k)], "Oy", turn(y, k))

    GCs[...] = dot_nt(OG[pl.ds(2 * oc, 2)].reshape(128, -1), wd[...]).reshape(GCs.shape)
    send(GCs, GCr, core, "Gc", 0)
    GOWN[...] = dot_nt(OG[pl.ds(2 * c, 2)].reshape(128, -1), wd[...]).reshape(GOWN.shape)
    arrive(GCr, "Gc", 0)
    for k in KS:
        v = turn(x, k)
        GXs[v] = (GOWN[v] + GCr[v]).astype(BF)
        send(GXs.at[v], GXr.at[x], x_dev(v), "Gx", x)
    gd_o[...] = dot_tn(HID[...].reshape(16 * ROWS, -1), OG[...].reshape(16 * ROWS, -1)).astype(BF)
    for k in KS:
        arrive(GXr.at[turn(x, k)], "Gx", turn(x, k))
    total = GOWN[x] + GCr[x]
    for k in KS:
        total = total + GXr[turn(x, k)].astype(F32)
    GZ[zl] = total.astype(BF)
    for k in KS:
        send(GZ.at[zl], GZ.at[zl], zl_dev(turn(zl, k)), "Gzl", zl)
    for w in range(4):
        arrive(AB.at[oc, w], "ABc", w)
    for k in KS:
        arrive(GZ.at[turn(zl, k)], "Gzl", turn(zl, k))
    total = GZ[0].astype(F32)
    for w in range(1, 4):
        total = total + GZ[w].astype(F32)
    HG[c, x] = total.astype(BF)
    for k in KS:
        send(HG.at[c, x], HG.at[c, x], x_dev(turn(x, k)), "Gax", x)
    send(HG.at[c, x], HG.at[c, x], core, "Gac", x)
    for k in KS:
        v = turn(x, k)
        arrive(HG.at[c, v], "Gax", v)
        send(HG.at[c, v], HG.at[c, v], core, "Gac", v)
    for w in range(4):
        arrive(HG.at[oc, w], "Gac", w)
    for cc in range(2):
        for v in range(4):
            g = HG[cc, v].astype(F32)
            GG[cc, v] = (g * AB[cc, v, 0].reshape(32, fs).astype(F32)).astype(BF)
            UG[cc, v] = (g * AB[cc, v, 1].reshape(32, fs).astype(F32)).astype(BF)

    gates, ups = GG[...].reshape(16 * ROWS, -1), UG[...].reshape(16 * ROWS, -1)
    part = (dot_nt(gates, wg[...]) + dot_nt(ups, wu[...])).reshape(IPf.shape)
    IPf[...] = part
    IPs[...] = part.astype(BF)
    for k in KS:
        v = turn(y, k)
        send(IPs.at[:, v], IPr.at[y], y_dev(v), "Iy", y)
    gg_o[...] = dot(XT[...], gates).astype(BF)
    for k in KS:
        arrive(IPr.at[turn(y, k)], "Iy", turn(y, k))
    for z in range(4):
        total = IPf[z, y]
        for k in KS:
            total = total + IPr[turn(y, k), z].astype(F32)
        IZf[z] = total
        IZs[z] = total.astype(BF)
    for k in KS:
        v = turn(zh, k)
        send(IZs.at[v], IZr.at[zh], zh_dev(v), "Iz", zh)
    gu_o[...] = dot(XT[...], ups).astype(BF)
    for k in KS:
        arrive(IZr.at[turn(zh, k)], "Iz", turn(zh, k))
    total = IZf[zh]
    for k in KS:
        total = total + IZr[turn(zh, k)].astype(F32)
    ig_o[...] = total.astype(BF)
    for copy in sent:
        copy.wait_send()


def body(
    teacher_hidden,
    teacher_down,
    scale_index,
    distill_proj,
    assignment,
    student_input,
    w_gate,
    w_up,
    w_down,
):
    tokens, ft = teacher_hidden.shape
    dt, ds = distill_proj.shape
    fs = w_gate.shape[1]
    scales = jnp.repeat(jnp.exp2(scale_index.astype(F32) - 3.0), ft // scale_index.shape[0])
    pad = ((0, ROWS - tokens), (0, 0))
    th = jnp.pad((teacher_hidden.astype(F32) * scales).astype(BF), pad)
    xin = jnp.pad(student_input, pad)
    place = (assignment // tokens) * ROWS + assignment % tokens
    place = jnp.pad(place.reshape(-1, tokens), ((0, 0), (0, ROWS - tokens)), constant_values=-1)
    perm = (place.reshape(2, 128, 1) == jnp.arange(16 * ROWS, dtype=jnp.int32)).astype(BF)

    def v(shape, dtype=BF):
        return pltpu.VMEM(shape, dtype)

    dp4 = (4, 4, ROWS)
    scratch = [
        v((ft, dt)), v((dt, ds)), v((ds, fs)), v((ds, fs)), v((fs, ds)), v(dp4 + (ft,)), v(dp4 + (ds,)), v((ds, 16 * ROWS)),
        v((2, 4, 32, fs), F32), v((2, 4, 32, fs), F32), v((2, 4, 32, fs), F32), v((4, 2, 32, fs)), v((4, 2, 32, fs)),
        v((4, 2, 16, 512), F32), v((4, 2, 16, 512)), v((4, 2, 16, 512)), v((4, 16, 512)), v((4, 2, 16, 512)),
        v((2, 4, 2, 16, fs)), v((2, 4, 2, 2, 16, fs)),
        v((4, 32, dt), F32), v((4, 32, dt), F32), v((4, 32, dt), F32), v((4, 32, dt)), v((4, 32, dt)), v((4, 32, dt)), v((2, 4, 32, dt)),
        v((8, 128), F32), v((4, 8, 128), F32), v((4, 8, 128), F32), v((4, 8, 128), F32), v((2, 8, 128), F32),
        v(dp4 + (ds,), F32), v(dp4 + (ds,), F32), v(dp4 + (ds,), F32), v(dp4 + (ds,), F32),
        v(dp4 + (ds,)), v(dp4 + (ds,)),
        v((4, 32, fs), F32), v((4, 32, fs), F32), v((4, 32, fs), F32), v((4, 32, fs)), v((4, 32, fs)), v((4, 32, fs)),
        v((2, 4, 32, fs)), v((2, 4, 32, fs)), v((2, 4, 32, fs)),
        v(dp4 + (ds,), F32), v(dp4 + (ds,)), v(dp4 + (ds,)), v((4, ROWS, ds), F32), v((4, ROWS, ds)), v((4, ROWS, ds)),
        pltpu.SemaphoreType.DMA((N_SEND,)), pltpu.SemaphoreType.DMA((N_RECV,)), pltpu.SemaphoreType.DMA((5,)),
    ]
    vm, hbm = pl.BlockSpec(memory_space=pltpu.VMEM), pl.BlockSpec(memory_space=pl.ANY)
    sds = jax.ShapeDtypeStruct
    grad_gate, grad_up, grad_down, input_grad = pl.pallas_call(
        kernel,
        out_shape=(sds((ds, fs), BF), sds((ds, fs), BF), sds((fs, ds), BF), sds((ROWS, ds), BF)),
        in_specs=[vm] * 3 + [hbm] * 5,
        out_specs=(vm,) * 4,
        scratch_shapes=scratch,
        compiler_params=pltpu.CompilerParams(collective_id=0, has_side_effects=True, vmem_limit_bytes=56 << 20),
        name="distill_step",
    )(th, xin, perm, teacher_down, distill_proj, w_gate, w_up, w_down)
    return grad_gate, grad_up, grad_down, input_grad[:tokens]


def solution(mesh):
    placed = (
        P("dp", "mp"),
        P("mp", "dp"),
        P("mp"),
        P("dp", "mp"),
        P(),
        P("dp", "mp"),
        P("mp", "dp"),
        P("mp", "dp"),
        P("dp", "mp"),
    )
    return jax.shard_map(
        body,
        mesh=mesh,
        in_specs=placed,
        out_specs=(P("mp", "dp"), P("mp", "dp"), P("dp", "mp"), P("dp", "mp")),
        check_vma=False,
    )
```

time: 1020 us -> 128 us (0.13)
  the two profiles are of different devices: /device:TPU:1 before, /device:TPU:64 now
where the time goes in v1:
time: 128 us; the launch traced here: 127 us
  Pallas kernels  117 us (91%)
  local copies, waits for them, and re-layouts  7.31 us (6%)
  other arithmetic  2.88 us (2%)
    pallas_call x1, Pallas kernels, body(): pl.pallas_call(kernel, out_shape=(sds((ds, fs), BF), sds((ds, fs), BF), s...  117 us
    unnamed x8, local copies, waits for them, and re-layouts  5.07 us

profile of v1, /device:TPU:64, one launch (start us, length us, event | category | flops | bytes accessed | tf_op | source)
XLA Modules:
  0.0 127.4 jit_solution(12298161769020827143)
XLA Ops:
  0.6 0.7 multiply_exponential_fusion
  1.3 0.7 fusion.1
  2.0 0.1 reshape.14
  2.1 0.1 eq.17
  2.2 0.1 broadcast_in_dim.4
  2.2 0.1 mul.16
  2.3 1.3 %pad.13.xin = bf16[16,256]{1,0:T(8,128)(2,1)} pad(bf16[14,256]{1,0:T(8,128)(2,1)} %param.14, bf16[]{:T(256)} %constant.25.clone.1), padding=0_2x0_0 | pad | bytes 15362 | tf_op jit(solution)/shard_map/jit(_pad)/pad | solution.py:383
  3.6 0.8 multiply_convert_fusion
  4.4 0.6 pad.12.th
  5.0 0.8 fusion.perm
  5.8 116.5 %distill_step.1 = (bf16[256,896]{1,0:T(8,128)(2,1)}, bf16[256,896]{1,0:T(8,128)(2,1)}, bf16[896,256]{1,0:T(8,128)(2,1)}, bf16[16,256]{1,0:T(8,128)(2,1)}) custom-call(bf16[16,832]{1,0:T(8,128)(2,1)} %pad.12.th, bf16[16,256]{1,0:T(8,128)(2,1)} %pad.13.xin, bf16[2,128,256]{2,1,0:T(8,128)(2,1)} %fusion.perm, bf16[832,1024]{1,0:T(8,128)(2,1)} %td_h.1, ...), custom_call_target="tpu_custom_call" | custom-call | tf_op jit(solution)/shard_map/distill_step/pallas_call | solution.py:408
  122.3 0.0 copy-start
  122.3 0.0 copy-start.1
  122.3 1.9 %copy.17 = bf16[256,896]{1,0:T(8,128)(2,1)} copy(bf16[256,896]{1,0:T(8,128)(2,1)} %get-tuple-element.16) | data formatting | bytes 917504
  124.2 1.8 %copy.18 = bf16[256,896]{1,0:T(8,128)(2,1)} copy(bf16[256,896]{1,0:T(8,128)(2,1)} %get-tuple-element.17) | data formatting | bytes 917504
  126.0 0.0 copy-done
  126.0 0.8 copy.19
  126.8 0.0 copy-done.1
  126.8 0.6 copy.20
  (1 shorter events, 0.0 us)
Async XLA Ops:
  122.3 3.7 %copy-start = (bf16[896,256]{1,0:T(8,128)(2,1)S(1)}, bf16[896,256]{1,0:T(8,128)(2,1)}, u32[]{:S(2)}) copy-start(bf16[896,256]{1,0:T(8,128)(2,1)} %get-tuple-element.18) | copy-start | bytes 1376260
  122.3 4.5 %copy-start.1 = (bf16[16,256]{1,0:T(8,128)(2,1)S(1)}, bf16[16,256]{1,0:T(8,128)(2,1)}, u32[]{:S(2)}) copy-start(bf16[16,256]{1,0:T(8,128)(2,1)} %get-tuple-element.11) | copy-start | bytes 24580

commit v2 on v1

v2 whole, which is shorter than its diff:
```python
import functools

import jax
import jax.numpy as jnp
from jax import lax
from jax.experimental import pallas as pl
from jax.experimental.pallas import tpu as pltpu
from jax.sharding import PartitionSpec as P

MESH = pl.DeviceIdType.MESH
BF, F32 = jnp.bfloat16, jnp.float32
ROWS = 16
KS = (2, 1, 3)

RECV = {}
N_RECV = 0
for _name, _n in (
    ("Sz", 4), ("Sy", 16), ("Tz", 4), ("Ty", 16), ("Sc", 2), ("Tc", 2), ("Sx", 8), ("Tx", 8), ("Szl", 8), ("Tzl", 8),
    ("Hzl", 4), ("ABzl", 4), ("Hx", 4), ("Hc", 4), ("ABx", 4), ("ABc", 4), ("Tax", 8), ("Tac", 8),
    ("Md", 16), ("Mc", 8), ("TPy", 4), ("SPy", 4), ("Oz", 4), ("Oy", 4),
    ("Gc", 2), ("Gx", 8), ("Gzl", 8), ("Gax", 8), ("Gac", 8), ("Iy", 4), ("Iz", 4),
):
    RECV[_name] = N_RECV
    N_RECV += _n
N_SEND = 170


def dot(a, b):
    return jnp.dot(a, b, preferred_element_type=F32)


def dot_nt(a, b):
    return lax.dot_general(a, b, (((1,), (1,)), ((), ())), preferred_element_type=F32)


def dot_tn(a, b):
    return lax.dot_general(a, b, (((0,), (0,)), ((), ())), preferred_element_type=F32)


def kernel(
    index, assign, th, xin, td_h, dp_h, wg_h, wu_h, wd_h,
    gg_o, gu_o, gd_o, ig_o,
    td, dpj, wg, wu, wd, perm, TG, XG, XT,
    SCs, SCr, SOWN, SXs, SXr, SZf, SZs, SZr, HZ, ABZ, HID, AB,
    TCs, TCr, TOWN, TXs, TXr, TZ, TO, AMd, AMc,
    TPf, TPr, SPf, SPr, OZ, OG,
    GCs, GCr, GOWN, GXs, GXr, GZ, HG, GG, UG, IPf, IPs, IPr, IZf, IZs, IZr,
    send_sem, recv_sem, load_sem,
):
    d, m = lax.axis_index("dp"), lax.axis_index("mp")
    zh, y, zl, x, c = d // 4, d % 4, m // 8, (m // 2) % 4, m % 2
    oc = 1 - c

    def turn(v, k):
        return lax.rem(v + k, 4)

    def at(zh=zh, y=y, zl=zl, x=x, c=c):
        return (zh * 4 + y, zl * 8 + x * 2 + c)

    core = at(c=oc)
    x_dev = lambda v: at(x=v)
    y_dev = lambda v: at(y=v)
    zl_dev = lambda v: at(zl=v)
    zh_dev = lambda v: at(zh=v)

    sent = []

    def send(src, dst, dev, name, slot):
        copy = pltpu.make_async_remote_copy(
            src, dst, send_sem.at[len(sent)], recv_sem.at[RECV[name] + slot], device_id=dev, device_id_type=MESH
        )
        copy.start()
        sent.append(copy)

    def arrive(dst, name, slot):
        pltpu.make_async_remote_copy(
            dst, dst, send_sem.at[0], recv_sem.at[RECV[name] + slot], device_id=core, device_id_type=MESH
        ).wait_recv()

    def scatter_x(own, other, out, into, n_core, n_x, r):
        arrive(other.at[:, r], n_core, r)
        for k in KS:
            v = turn(x, k)
            out[v, r] = (own[v, r] + other[v, r]).astype(BF)
            send(out.at[v, r], into.at[x, r], x_dev(v), n_x, x * 2 + r)

    def share_zl(own, other, into, shares, n_x, n_zl, r):
        total = own[x, r] + other[x, r]
        for k in KS:
            arrive(into.at[turn(x, k), r], n_x, turn(x, k) * 2 + r)
        for k in KS:
            total = total + into[turn(x, k), r].astype(F32)
        shares[zl, r] = total.astype(BF)
        for k in KS:
            send(shares.at[zl, r], shares.at[zl, r], zl_dev(turn(zl, k)), n_zl, zl * 2 + r)

    def gather_x(shares, result, n_zl, n_x, n_core, r):
        for k in KS:
            arrive(shares.at[turn(zl, k), r], n_zl, turn(zl, k) * 2 + r)
        total = shares[0, r].astype(F32)
        for w in range(1, 4):
            total = total + shares[w, r].astype(F32)
        result[c, x, r] = total.astype(BF)
        mine = result.at[c, x, r]
        for k in KS:
            send(mine, mine, x_dev(turn(x, k)), n_x, x * 2 + r)
        send(mine, mine, core, n_core, x * 2 + r)

    def pass_on(result, n_x, n_core, r):
        for k in KS:
            v = turn(x, k)
            arrive(result.at[c, v, r], n_x, v * 2 + r)
            send(result.at[c, v, r], result.at[c, v, r], core, n_core, v * 2 + r)

    barrier = pltpu.get_barrier_semaphore()
    partners = [core]
    for k in KS:
        partners += [x_dev(turn(x, k)), at(x=turn(x, k), c=oc), zl_dev(turn(zl, k))]
    dp_group = [at(zh=turn(zh, i), y=turn(y, j)) for i in KS + (0,) for j in KS + (0,)][:-1]
    pairs = [at(x=turn(x, k), c=b) for k in KS for b in (oc, c)] + [core]
    partners += dp_group
    for p in partners:
        pl.semaphore_signal(barrier, inc=1, device_id=p, device_id_type=MESH)
    loads = [
        pltpu.make_async_copy(a, b, load_sem.at[i])
        for i, (a, b) in enumerate(((wg_h, wg), (wu_h, wu), (td_h, td), (dp_h, dpj), (wd_h, wd)))
    ]
    for load in loads:
        load.start()
    tokens, ft = th.shape
    groups = index.shape[0]

    def padded(rows):
        return jnp.concatenate([rows, jnp.zeros((ROWS - tokens, rows.shape[1]), F32)], axis=0).astype(BF)

    XG[zh, y] = padded(xin[...].astype(F32))
    group = lax.broadcasted_iota(jnp.int32, (1, ft), 1) // (ft // groups)
    level = jnp.zeros((1, ft), jnp.int32)
    for i in range(groups):
        level = jnp.where(group == i, index[i], level)
    scales = jnp.full((1, ft), 0.125, F32)
    for i in range(1, 7):
        scales = jnp.where(level == i, 0.125 * 2**i, scales)
    TG[zh, y] = padded(th[...].astype(F32) * scales)

    def place(block, carry):
        row = lax.broadcasted_iota(jnp.int32, (ROWS, 16 * ROWS), 0)
        column = lax.broadcasted_iota(jnp.int32, (ROWS, 16 * ROWS), 1)
        source = jnp.full((ROWS, 16 * ROWS), -1, jnp.int32)
        for i in range(tokens):
            a = assign[block * tokens + i]
            source = jnp.where(row == i, lax.div(a, tokens) * ROWS + lax.rem(a, tokens), source)
        perm[block] = jnp.where(source == column, 1.0, 0.0).astype(BF)
        return carry

    lax.fori_loop(0, 16, place, 0)
    pl.semaphore_wait(barrier, len(partners))

    for buf, nz, ny in ((XG, "Sz", "Sy"), (TG, "Tz", "Ty")):
        own = buf.at[zh, y]
        for k in KS:
            send(own, own, zh_dev(turn(zh, k)), nz, zh)
        for k in KS:
            send(own, own, y_dev(turn(y, k)), ny, zh * 4 + y)
    for buf, nz, ny in ((XG, "Sz", "Sy"), (TG, "Tz", "Ty")):
        for k in KS:
            z = turn(zh, k)
            arrive(buf.at[z, y], nz, z)
            for j in KS:
                send(buf.at[z, y], buf.at[z, y], y_dev(turn(y, j)), ny, z * 4 + y)

    for j in KS:
        for z in range(4):
            arrive(XG.at[z, turn(y, j)], "Sy", z * 4 + turn(y, j))
    loads[0].wait()
    loads[1].wait()
    half = XG[pl.ds(2 * oc, 2)].reshape(128, -1)
    for a, w in enumerate((wg, wu)):
        SCs[a] = dot(half, w[...]).reshape(SCs.shape[1:])
        send(SCs.at[a], SCr.at[a], core, "Sc", a)
    half = XG[pl.ds(2 * c, 2)].reshape(128, -1)
    for a, w in enumerate((wg, wu)):
        SOWN[a] = dot(half, w[...]).reshape(SOWN.shape[1:])

    for j in KS:
        for z in range(4):
            arrive(TG.at[z, turn(y, j)], "Ty", z * 4 + turn(y, j))
    loads[2].wait()
    everything = TG[...].reshape(16 * ROWS, -1)
    picked = dot(perm[pl.ds(8 * oc, 8)].reshape(128, -1), everything).astype(BF)
    TCs[...] = dot(picked, td[...]).reshape(TCs.shape)
    for r in range(2):
        send(TCs.at[:, r], TCr.at[:, r], core, "Tc", r)
    picked = dot(perm[pl.ds(8 * c, 8)].reshape(128, -1), everything).astype(BF)
    TOWN[...] = dot(picked, td[...]).reshape(TOWN.shape)

    for a in range(2):
        arrive(SCr.at[a], "Sc", a)
        for k in KS:
            v = turn(x, k)
            SXs[v, a] = (SOWN[a, v] + SCr[a, v]).astype(BF)
            send(SXs.at[v, a], SXr.at[x, a], x_dev(v), "Sx", x * 2 + a)
    for r in range(2):
        scatter_x(TOWN, TCr, TXs, TXr, "Tc", "Tx", r)
    XT[...] = XG[...].reshape(16 * ROWS, -1).T

    fs = SOWN.shape[-1]
    shift = fs - 512
    for a in range(2):
        for k in KS:
            arrive(SXr.at[turn(x, k), a], "Sx", turn(x, k) * 2 + a)
        total = SOWN[a, x] + SCr[a, x]
        for k in KS:
            total = total + SXr[turn(x, k), a].astype(F32)
        for w in range(4):
            r, h = w % 2, w // 2
            part = total[r * 16 : r * 16 + 16, h * shift : h * shift + 512]
            SZf[w, a] = part
            SZs[w, a] = part.astype(BF)
        for k in KS:
            v = turn(zl, k)
            send(SZs.at[v, a], SZr.at[zl, a], zl_dev(v), "Szl", zl * 2 + a)
    for r in range(2):
        share_zl(TOWN, TCr, TXr, TZ, "Tx", "Tzl", r)

    pre = []
    for a in range(2):
        for k in KS:
            arrive(SZr.at[turn(zl, k), a], "Szl", turn(zl, k) * 2 + a)
        total = SZf[zl, a]
        for k in KS:
            total = total + SZr[turn(zl, k), a].astype(F32)
        pre.append(total)
    gate, up = pre
    sig = jax.nn.sigmoid(gate)
    HZ[zl] = (gate * sig * up).astype(BF)
    for k in KS:
        send(HZ.at[zl], HZ.at[zl], zl_dev(turn(zl, k)), "Hzl", zl)
    ABZ[zl, 0] = (up * sig * (1.0 + gate * (1.0 - sig))).astype(BF)
    ABZ[zl, 1] = (gate * sig).astype(BF)
    for k in KS:
        send(ABZ.at[zl], ABZ.at[zl], zl_dev(turn(zl, k)), "ABzl", zl)

    for r in range(2):
        gather_x(TZ, TO, "Tzl", "Tax", "Tac", r)
    AMd[zh, y] = jnp.full((8, 128), jnp.max(jnp.abs(TO[c, x].astype(F32))), F32)
    for p in dp_group:
        send(AMd.at[zh, y], AMd.at[zh, y], p, "Md", zh * 4 + y)

    for k in KS:
        arrive(HZ.at[turn(zl, k)], "Hzl", turn(zl, k))
    for r in range(2):
        HID[c, x, r, :, 0:512] = HZ[r]
        HID[c, x, r, :, 512:fs] = HZ[2 + r][:, 512 - shift :]
    for k in KS:
        send(HID.at[c, x], HID.at[c, x], x_dev(turn(x, k)), "Hx", x)
    send(HID.at[c, x], HID.at[c, x], core, "Hc", x)

    for r in range(2):
        pass_on(TO, "Tax", "Tac", r)
    for k in KS:
        v = turn(x, k)
        arrive(HID.at[c, v], "Hx", v)
        send(HID.at[c, v], HID.at[c, v], core, "Hc", v)

    loads[3].wait()
    for w in range(8):
        arrive(TO.at[oc, w // 2, w % 2], "Tac", w)
    part = dot(TO[...].reshape(16 * ROWS, -1), dpj[...]).reshape(TPf.shape)
    TPf[...] = part
    for k in KS:
        v = turn(y, k)
        send(TPf.at[:, v], TPr.at[y], y_dev(v), "TPy", y)
    loads[4].wait()
    for w in range(4):
        arrive(HID.at[oc, w], "Hc", w)
    part = dot(HID[...].reshape(16 * ROWS, -1), wd[...]).reshape(SPf.shape)
    SPf[...] = part
    for k in KS:
        v = turn(y, k)
        send(SPf.at[:, v], SPr.at[y], y_dev(v), "SPy", y)

    for i in KS + (0,):
        for j in KS + (0,):
            if i or j:
                arrive(AMd.at[turn(zh, i), turn(y, j)], "Md", turn(zh, i) * 4 + turn(y, j))
    AMc[x, c] = jnp.max(AMd[...].reshape(16, 8, 128), axis=0)
    for p in pairs:
        send(AMc.at[x, c], AMc.at[x, c], p, "Mc", x * 2 + c)
    for k in KS:
        arrive(ABZ.at[turn(zl, k)], "ABzl", turn(zl, k))
    for a in range(2):
        for r in range(2):
            AB[c, x, a, r, :, 0:512] = ABZ[r, a]
            AB[c, x, a, r, :, 512:fs] = ABZ[2 + r, a][:, 512 - shift :]
    for k in KS:
        send(AB.at[c, x], AB.at[c, x], x_dev(turn(x, k)), "ABx", x)
    send(AB.at[c, x], AB.at[c, x], core, "ABc", x)

    for k in KS:
        arrive(TPr.at[turn(y, k)], "TPy", turn(y, k))
        arrive(SPr.at[turn(y, k)], "SPy", turn(y, k))
    for k in KS:
        for b in range(2):
            arrive(AMc.at[turn(x, k), b], "Mc", turn(x, k) * 2 + b)
    arrive(AMc.at[x, oc], "Mc", x * 2 + oc)
    scale = (4.0 / jnp.max(AMc[...].reshape(8, 8, 128), axis=0))[0:1, 0:1]
    for z in range(4):
        target, student = TPf[z, y], SPf[z, y]
        for k in KS:
            target = target + TPr[turn(y, k), z]
            student = student + SPr[turn(y, k), z]
        OZ[zh, z] = ((student - target * scale) * 0.5).astype(BF)
    for k in KS:
        send(OZ.at[zh], OZ.at[zh], zh_dev(turn(zh, k)), "Oz", zh)
    for k in KS:
        v = turn(x, k)
        arrive(AB.at[c, v], "ABx", v)
        send(AB.at[c, v], AB.at[c, v], core, "ABc", v)
    for k in KS:
        arrive(OZ.at[turn(zh, k)], "Oz", turn(zh, k))
    for z in range(4):
        total = OZ[0, z].astype(F32)
        for w in range(1, 4):
            total = total + OZ[w, z].astype(F32)
        OG[z, y] = total.astype(BF)
    for k in KS:
        send(OG.at[:, y], OG.at[:, y], y_dev(turn(y, k)), "Oy", y)
    for k in KS:
        arrive(OG.at[:, turn(y, k)], "Oy", turn(y, k))

    GCs[...] = dot_nt(OG[pl.ds(2 * oc, 2)].reshape(128, -1), wd[...]).reshape(GCs.shape)
    for r in range(2):
        send(GCs.at[:, r], GCr.at[:, r], core, "Gc", r)
    GOWN[...] = dot_nt(OG[pl.ds(2 * c, 2)].reshape(128, -1), wd[...]).reshape(GOWN.shape)
    for r in range(2):
        scatter_x(GOWN, GCr, GXs, GXr, "Gc", "Gx", r)
    gd_o[...] = dot_tn(HID[...].reshape(16 * ROWS, -1), OG[...].reshape(16 * ROWS, -1)).astype(BF)
    for r in range(2):
        share_zl(GOWN, GCr, GXr, GZ, "Gx", "Gzl", r)
    for w in range(4):
        arrive(AB.at[oc, w], "ABc", w)
    for r in range(2):
        gather_x(GZ, HG, "Gzl", "Gax", "Gac", r)
    for r in range(2):
        pass_on(HG, "Gax", "Gac", r)
    for w in range(8):
        arrive(HG.at[oc, w // 2, w % 2], "Gac", w)
    for cc in range(2):
        for v in range(4):
            g = HG[cc, v].astype(F32)
            GG[cc, v] = (g * AB[cc, v, 0].astype(F32)).astype(BF)
            UG[cc, v] = (g * AB[cc, v, 1].astype(F32)).astype(BF)

    gates, ups = GG[...].reshape(16 * ROWS, -1), UG[...].reshape(16 * ROWS, -1)
    part = (dot_nt(gates, wg[...]) + dot_nt(ups, wu[...])).reshape(IPf.shape)
    IPf[...] = part
    IPs[...] = part.astype(BF)
    for k in KS:
        v = turn(y, k)
        send(IPs.at[:, v], IPr.at[y], y_dev(v), "Iy", y)
    gg_o[...] = dot(XT[...], gates).astype(BF)
    for k in KS:
        arrive(IPr.at[turn(y, k)], "Iy", turn(y, k))
    for z in range(4):
        total = IPf[z, y]
        for k in KS:
            total = total + IPr[turn(y, k), z].astype(F32)
        IZf[z] = total
        IZs[z] = total.astype(BF)
    for k in KS:
        v = turn(zh, k)
        send(IZs.at[v], IZr.at[zh], zh_dev(v), "Iz", zh)
    gu_o[...] = dot(XT[...], ups).astype(BF)
    for k in KS:
        arrive(IZr.at[turn(zh, k)], "Iz", turn(zh, k))
    total = IZf[zh]
    for k in KS:
        total = total + IZr[turn(zh, k)].astype(F32)
    ig_o[...] = total.astype(BF)
    for copy in sent:
        copy.wait_send()


def hand_over(gg, gu, gd, ig, gg_o, gu_o, gd_o, ig_o, gg_v, gu_v, gd_v, sem):
    ways = ((gg, gg_v, gg_o), (gu, gu_v, gu_o), (gd, gd_v, gd_o))
    loads = [pltpu.make_async_copy(a, b, sem.at[0, i]) for i, (a, b, _) in enumerate(ways)]
    stores = [pltpu.make_async_copy(b, o, sem.at[1, i]) for i, (_, b, o) in enumerate(ways)]
    for load in loads:
        load.start()
    ig_o[...] = ig[...].astype(F32)[: ig_o.shape[0]].astype(BF)
    for load, store in zip(loads, stores):
        load.wait()
        store.start()
    for store in stores:
        store.wait()


def body(
    teacher_hidden,
    teacher_down,
    scale_index,
    distill_proj,
    assignment,
    student_input,
    w_gate,
    w_up,
    w_down,
):
    tokens, ft = teacher_hidden.shape
    dt, ds = distill_proj.shape
    fs = w_gate.shape[1]

    def v(shape, dtype=BF):
        return pltpu.VMEM(shape, dtype)

    dp4 = (4, 4, ROWS)
    scratch = [
        v((ft, dt)), v((dt, ds)), v((ds, fs)), v((ds, fs)), v((fs, ds)), v((16, ROWS, 16 * ROWS)), v(dp4 + (ft,)), v(dp4 + (ds,)), v((ds, 16 * ROWS)),
        v((2, 4, 32, fs), F32), v((2, 4, 32, fs), F32), v((2, 4, 32, fs), F32), v((4, 2, 32, fs)), v((4, 2, 32, fs)),
        v((4, 2, 16, 512), F32), v((4, 2, 16, 512)), v((4, 2, 16, 512)), v((4, 16, 512)), v((4, 2, 16, 512)),
        v((2, 4, 2, 16, fs)), v((2, 4, 2, 2, 16, fs)),
        v((4, 2, 16, dt), F32), v((4, 2, 16, dt), F32), v((4, 2, 16, dt), F32), v((4, 2, 16, dt)), v((4, 2, 16, dt)),
        v((4, 2, 16, dt)), v((2, 4, 2, 16, dt)),
        v((4, 4, 8, 128), F32), v((4, 2, 8, 128), F32),
        v(dp4 + (ds,), F32), v(dp4 + (ds,), F32), v(dp4 + (ds,), F32), v(dp4 + (ds,), F32),
        v(dp4 + (ds,)), v(dp4 + (ds,)),
        v((4, 2, 16, fs), F32), v((4, 2, 16, fs), F32), v((4, 2, 16, fs), F32), v((4, 2, 16, fs)), v((4, 2, 16, fs)),
        v((4, 2, 16, fs)), v((2, 4, 2, 16, fs)), v((2, 4, 2, 16, fs)), v((2, 4, 2, 16, fs)),
        v(dp4 + (ds,), F32), v(dp4 + (ds,)), v(dp4 + (ds,)), v((4, ROWS, ds), F32), v((4, ROWS, ds)), v((4, ROWS, ds)),
        pltpu.SemaphoreType.DMA((N_SEND,)), pltpu.SemaphoreType.DMA((N_RECV,)), pltpu.SemaphoreType.DMA((5,)),
    ]
    vm, hbm = pl.BlockSpec(memory_space=pltpu.VMEM), pl.BlockSpec(memory_space=pl.ANY)
    sm = pl.BlockSpec(memory_space=pltpu.SMEM)
    sds = jax.ShapeDtypeStruct
    grad_gate, grad_up, grad_down, input_grad = pl.pallas_call(
        kernel,
        out_shape=(sds((ds, fs), BF), sds((ds, fs), BF), sds((fs, ds), BF), sds((ROWS, ds), BF)),
        in_specs=[sm] * 2 + [vm] * 2 + [hbm] * 5,
        out_specs=(vm,) * 4,
        scratch_shapes=scratch,
        compiler_params=pltpu.CompilerParams(collective_id=0, has_side_effects=True, vmem_limit_bytes=56 << 20),
        name="distill_step",
    )(scale_index, assignment, teacher_hidden, student_input, teacher_down, distill_proj, w_gate, w_up, w_down)
    return pl.pallas_call(
        hand_over,
        out_shape=(sds((ds, fs), BF), sds((ds, fs), BF), sds((fs, ds), BF), sds((tokens, ds), BF)),
        in_specs=[hbm] * 3 + [vm],
        out_specs=(hbm,) * 3 + (vm,),
        scratch_shapes=[v((ds, fs)), v((ds, fs)), v((fs, ds)), pltpu.SemaphoreType.DMA((2, 3))],
        name="hand_over",
    )(grad_gate, grad_up, grad_down, input_grad)


def solution(mesh):
    placed = (
        P("dp", "mp"),
        P("mp", "dp"),
        P("mp"),
        P("dp", "mp"),
        P(),
        P("dp", "mp"),
        P("mp", "dp"),
        P("mp", "dp"),
        P("dp", "mp"),
    )
    return jax.shard_map(
        body,
        mesh=mesh,
        in_specs=placed,
        out_specs=(P("mp", "dp"), P("mp", "dp"), P("dp", "mp"), P("dp", "mp")),
        check_vma=False,
    )
```

time: 128 us -> 116 us (0.906)
  the two profiles are of different devices: /device:TPU:64 before, /device:TPU:1 now
where the time goes in v2:
time: 116 us
  Pallas kernels  115 us (99%)
    pallas_call x1, Pallas kernels, body(): pl.pallas_call(kernel, out_shape=(sds((ds, fs), BF), sds((ds, fs), BF), s...  112 us
    pallas_call x1, Pallas kernels, body(): pl.pallas_call(hand_over, out_shape=(sds((ds, fs), BF), sds((ds, fs), BF)...  3.43 us

profile of v2, /device:TPU:1, one launch (start us, length us, event | category | flops | bytes accessed | tf_op | source)
XLA Modules:
  0.0 116.1 jit_solution(12583214331580061427)
XLA Ops:
  0.6 112.0 %distill_step.1 = (bf16[256,896]{1,0:T(8,128)(2,1)}, bf16[256,896]{1,0:T(8,128)(2,1)}, bf16[896,256]{1,0:T(8,128)(2,1)}, bf16[16,256]{1,0:T(8,128)(2,1)}) custom-call(s32[13]{0:T(128)} %index.1, s32[224]{0:T(256)} %assign.1, bf16[14,832]{1,0:T(8,128)(2,1)} %th.1, bf16[14,256]{1,0:T(8,128)(2,1)} %xin.1, bf16[832,1024]{1,0:T(8,128)(2,1)} %td_h.1, ...), custom_call_target="tpu_custom_call" | custom-call | tf_op jit(solution)/shard_map/distill_step/pallas_call | solution.py:436
  112.6 3.4 %hand_over.1 = (bf16[256,896]{1,0:T(8,128)(2,1)}, bf16[256,896]{1,0:T(8,128)(2,1)}, bf16[896,256]{1,0:T(8,128)(2,1)}, bf16[14,256]{1,0:T(8,128)(2,1)}) custom-call(bf16[256,896]{1,0:T(8,128)(2,1)} %get-tuple-element.8.gg, bf16[256,896]{1,0:T(8,128)(2,1)} %get-tuple-element.9.gu, bf16[896,256]{1,0:T(8,128)(2,1)} %get-tuple-element.10.gd, ...), custom_call_target="tpu_custom_call" | custom-call | tf_op jit(solution)/shard_map/hand_over/pallas_call | solution.py:445

commit v3 on v2

v3 whole, which is shorter than its diff:
```python
import functools

import jax
import jax.numpy as jnp
from jax import lax
from jax.experimental import pallas as pl
from jax.experimental.pallas import tpu as pltpu
from jax.sharding import PartitionSpec as P

MESH = pl.DeviceIdType.MESH
BF, F32 = jnp.bfloat16, jnp.float32
ROWS = 16
KS = (2, 1, 3)

RECV = {}
N_RECV = 0
for _name, _n in (
    ("Sz", 4), ("Tz", 4), ("Sy", 4), ("Ty", 4), ("Sc", 2), ("Tc", 2), ("Sx", 8), ("Tx", 8), ("Szl", 8), ("Tzl", 8), ("Tzg", 8),
    ("Hzl", 4), ("ABzl", 4), ("Hx", 4), ("Hc", 1), ("ABx", 4), ("ABc", 1), ("Tax", 8), ("Tac", 1),
    ("Md", 16), ("Mc", 8), ("TPy", 4), ("SPy", 4), ("Iz", 4),
):
    RECV[_name] = N_RECV
    N_RECV += _n
for _name, _earlier in (
    ("Oz", "Sz"), ("Oy", "Sy"), ("Gc", "Tc"), ("Gx", "Tx"), ("Gzl", "Tzl"), ("Gax", "Tax"), ("Gac", "Tac"), ("Iy", "Md"),
):
    RECV[_name] = RECV[_earlier]
N_SEND = 48


def dot(a, b):
    return jnp.dot(a, b, preferred_element_type=F32)


def dot_nt(a, b):
    return lax.dot_general(a, b, (((1,), (1,)), ((), ())), preferred_element_type=F32)


def dot_tn(a, b):
    return lax.dot_general(a, b, (((0,), (0,)), ((), ())), preferred_element_type=F32)


def kernel(
    index_h, assign_h, th_h, xin_h, td_h, dp_h, wg_h, wu_h, wd_h,
    gg_h, gu_h, gd_h, ig_h,
    index, assign, th, xin, gg_o, gu_o, gd_o, ig_o,
    td, dpj, wg, wu, wd, perm, TG, XG, XT,
    SCs, SCr, SOWN, SXs, SXr, SZf, SZs, SZr, HZ, ABZ, HID, AB,
    TCs, TCr, TOWN, TXs, TXr, TZs, TZr, TW, TO, AMd, AMc,
    TPf, TPs, TPr, SPf, SPs, SPr, OZ, OG,
    GCs, GCr, GOWN, GXs, GXr, GZ, HG, GG, UG, IPf, IPs, IPr, IZs, IZr,
    send_sem, recv_sem, load_sem, store_sem,
):
    d, m = lax.axis_index("dp"), lax.axis_index("mp")
    zh, y, zl, x, c = d // 4, d % 4, m // 8, (m // 2) % 4, m % 2
    oc = 1 - c

    def turn(v, k):
        return lax.rem(v + k, 4)

    def at(zh=zh, y=y, zl=zl, x=x, c=c):
        return (zh * 4 + y, zl * 8 + x * 2 + c)

    core = at(c=oc)
    x_dev = lambda v: at(x=v)
    y_dev = lambda v: at(y=v)
    zl_dev = lambda v: at(zl=v)
    zh_dev = lambda v: at(zh=v)

    sent = []

    def send(src, dst, dev, name, slot):
        if len(sent) >= N_SEND:
            sent[-N_SEND].wait_send()
        copy = pltpu.make_async_remote_copy(
            src, dst, send_sem.at[len(sent) % N_SEND], recv_sem.at[RECV[name] + slot], device_id=dev, device_id_type=MESH
        )
        copy.start()
        sent.append(copy)

    def arrive(dst, name, slot):
        pltpu.make_async_remote_copy(
            dst, dst, send_sem.at[0], recv_sem.at[RECV[name] + slot], device_id=core, device_id_type=MESH
        ).wait_recv()

    def scatter_x(own, other, out, into, n_core, n_x, r):
        arrive(other.at[:, r], n_core, r)
        for k in KS:
            v = turn(x, k)
            out[v, r] = (own[v, r] + other[v, r].astype(F32)).astype(out.dtype)
            send(out.at[v, r], into.at[x, r], x_dev(v), n_x, x * 2 + r)

    def share_zl(own, other, into, shares, n_x, n_zl, r):
        total = own[x, r] + other[x, r].astype(F32)
        for k in KS:
            arrive(into.at[turn(x, k), r], n_x, turn(x, k) * 2 + r)
        for k in KS:
            total = total + into[turn(x, k), r].astype(F32)
        shares[zl, r] = total.astype(BF)
        for k in KS:
            send(shares.at[zl, r], shares.at[zl, r], zl_dev(turn(zl, k)), n_zl, zl * 2 + r)

    def gather_x(shares, result, n_zl, n_x, n_core, r):
        for k in KS:
            arrive(shares.at[turn(zl, k), r], n_zl, turn(zl, k) * 2 + r)
        total = shares[0, r].astype(F32)
        for w in range(1, 4):
            total = total + shares[w, r].astype(F32)
        result[c, x, r] = total.astype(BF)
        mine = result.at[c, x, r]
        for k in KS:
            send(mine, mine, x_dev(turn(x, k)), n_x, x * 2 + r)
        send(mine, mine, core, n_core, 0)

    def pass_on(result, n_x, n_core, r):
        for k in KS:
            v = turn(x, k)
            arrive(result.at[c, v, r], n_x, v * 2 + r)
            send(result.at[c, v, r], result.at[c, v, r], core, n_core, 0)

    barrier = pltpu.get_barrier_semaphore()
    partners = [core]
    for k in KS:
        partners += [x_dev(turn(x, k)), at(x=turn(x, k), c=oc), zl_dev(turn(zl, k))]
    dp_group = [at(zh=turn(zh, i), y=turn(y, j)) for i in KS + (0,) for j in KS + (0,)][:-1]
    pairs = [at(x=turn(x, k), c=b) for k in KS for b in (oc, c)] + [core]
    partners += dp_group
    for p in partners:
        pl.semaphore_signal(barrier, inc=1, device_id=p, device_id_type=MESH)
    loads = [
        pltpu.make_async_copy(a, b, load_sem.at[i])
        for i, (a, b) in enumerate(
            (
                (wg_h, wg), (wu_h, wu), (td_h, td), (dp_h, dpj), (wd_h, wd),
                (xin_h, xin), (index_h, index), (th_h, th), (assign_h, assign),
            )
        )
    ]
    for load in loads[5:] + loads[:5]:
        load.start()
    stores = []

    def store(src, dst):
        stores.append(pltpu.make_async_copy(src, dst, store_sem.at[len(stores)]))
        stores[-1].start()

    tokens, ft = th.shape
    groups = index.shape[0]

    def padded(rows):
        return jnp.concatenate([rows, jnp.zeros((ROWS - tokens, rows.shape[1]), F32)], axis=0).astype(BF)

    loads[5].wait()
    XG[zh, y] = padded(xin[...].astype(F32))
    group = lax.broadcasted_iota(jnp.int32, (1, ft), 1) // (ft // groups)
    level = jnp.zeros((1, ft), jnp.int32)
    loads[6].wait()
    for i in range(groups):
        level = jnp.where(group == i, index[i], level)
    scales = jnp.full((1, ft), 0.125, F32)
    for i in range(1, 7):
        scales = jnp.where(level == i, 0.125 * 2**i, scales)
    loads[7].wait()
    TG[zh, y] = padded(th[...].astype(F32) * scales)

    def place(block, carry):
        row = lax.broadcasted_iota(jnp.int32, (ROWS, 16 * ROWS), 0)
        column = lax.broadcasted_iota(jnp.int32, (ROWS, 16 * ROWS), 1)
        source = jnp.full((ROWS, 16 * ROWS), -1, jnp.int32)
        for i in range(tokens):
            a = assign[block * tokens + i]
            source = jnp.where(row == i, lax.div(a, tokens) * ROWS + lax.rem(a, tokens), source)
        perm[block] = jnp.where(source == column, 1.0, 0.0).astype(BF)
        return carry

    loads[8].wait()
    lax.fori_loop(0, 16, place, 0)
    pl.semaphore_wait(barrier, len(partners))

    for buf, nz, ny in ((XG, "Sz", "Sy"), (TG, "Tz", "Ty")):
        own = buf.at[zh, y]
        for k in KS:
            send(own, own, zh_dev(turn(zh, k)), nz, zh)
        for k in KS:
            send(own, own, y_dev(turn(y, k)), ny, y)
    for buf, nz, ny in ((XG, "Sz", "Sy"), (TG, "Tz", "Ty")):
        for k in KS:
            z = turn(zh, k)
            arrive(buf.at[z, y], nz, z)
            for j in KS:
                send(buf.at[z, y], buf.at[z, y], y_dev(turn(y, j)), ny, y)

    for j in KS:
        arrive(XG.at[:, turn(y, j)], "Sy", turn(y, j))
    loads[0].wait()
    loads[1].wait()
    half = XG[pl.ds(2 * oc, 2)].reshape(128, -1)
    for a, w in enumerate((wg, wu)):
        SCs[a] = dot(half, w[...]).reshape(SCs.shape[1:])
        send(SCs.at[a], SCr.at[a], core, "Sc", a)
    half = XG[pl.ds(2 * c, 2)].reshape(128, -1)
    for a, w in enumerate((wg, wu)):
        SOWN[a] = dot(half, w[...]).reshape(SOWN.shape[1:])

    for j in KS:
        arrive(TG.at[:, turn(y, j)], "Ty", turn(y, j))
    loads[2].wait()
    everything = TG[...].reshape(16 * ROWS, -1)
    picked = dot(perm[pl.ds(8 * oc, 8)].reshape(128, -1), everything).astype(BF)
    TCs[...] = dot(picked, td[...]).reshape(TCs.shape)
    for r in range(2):
        send(TCs.at[:, r], TCr.at[:, r], core, "Tc", r)
    picked = dot(perm[pl.ds(8 * c, 8)].reshape(128, -1), everything).astype(BF)
    TOWN[...] = dot(picked, td[...]).reshape(TOWN.shape)

    for a in range(2):
        arrive(SCr.at[a], "Sc", a)
        for k in KS:
            v = turn(x, k)
            SXs[v, a] = (SOWN[a, v] + SCr[a, v]).astype(BF)
            send(SXs.at[v, a], SXr.at[x, a], x_dev(v), "Sx", x * 2 + a)
    for r in range(2):
        scatter_x(TOWN, TCr, TXs, TXr, "Tc", "Tx", r)
    XT[...] = XG[...].reshape(16 * ROWS, -1).T

    fs = SOWN.shape[-1]
    shift = fs - 512
    for a in range(2):
        for k in KS:
            arrive(SXr.at[turn(x, k), a], "Sx", turn(x, k) * 2 + a)
        total = SOWN[a, x] + SCr[a, x]
        for k in KS:
            total = total + SXr[turn(x, k), a].astype(F32)
        for w in range(4):
            r, h = w % 2, w // 2
            part = total[r * 16 : r * 16 + 16, h * shift : h * shift + 512]
            SZf[w, a] = part
            SZs[w, a] = part.astype(BF)
        for k in KS:
            v = turn(zl, k)
            send(SZs.at[v, a], SZr.at[zl, a], zl_dev(v), "Szl", zl * 2 + a)
    piece = TZs.shape[-1]
    for r in range(2):
        total = TOWN[x, r] + TCr[x, r]
        for k in KS:
            arrive(TXr.at[turn(x, k), r], "Tx", turn(x, k) * 2 + r)
        for k in KS:
            total = total + TXr[turn(x, k), r]
        for w in range(4):
            TZs[w, r] = total[:, w * piece : (w + 1) * piece]
        for k in KS:
            v = turn(zl, k)
            send(TZs.at[v, r], TZr.at[zl, r], zl_dev(v), "Tzl", zl * 2 + r)

    pre = []
    for a in range(2):
        for k in KS:
            arrive(SZr.at[turn(zl, k), a], "Szl", turn(zl, k) * 2 + a)
        total = SZf[zl, a]
        for k in KS:
            total = total + SZr[turn(zl, k), a].astype(F32)
        pre.append(total)
    gate, up = pre
    sig = jax.nn.sigmoid(gate)
    HZ[zl] = (gate * sig * up).astype(BF)
    for k in KS:
        send(HZ.at[zl], HZ.at[zl], zl_dev(turn(zl, k)), "Hzl", zl)
    for r in range(2):
        total = TZs[zl, r]
        for k in KS:
            arrive(TZr.at[turn(zl, k), r], "Tzl", turn(zl, k) * 2 + r)
        for k in KS:
            total = total + TZr[turn(zl, k), r]
        TW[zl, r] = total.astype(BF)
        for k in KS:
            send(TW.at[zl, r], TW.at[zl, r], zl_dev(turn(zl, k)), "Tzg", zl * 2 + r)
    ABZ[zl, 0] = (up * sig * (1.0 + gate * (1.0 - sig))).astype(BF)
    ABZ[zl, 1] = (gate * sig).astype(BF)

    for k in KS:
        arrive(HZ.at[turn(zl, k)], "Hzl", turn(zl, k))
    for r in range(2):
        HID[c, x, r, :, 0:512] = HZ[r]
        HID[c, x, r, :, 512:fs] = HZ[2 + r][:, 512 - shift :]
    for k in KS:
        send(HID.at[c, x], HID.at[c, x], x_dev(turn(x, k)), "Hx", x)
    send(HID.at[c, x], HID.at[c, x], core, "Hc", 0)
    for r in range(2):
        for k in KS:
            arrive(TW.at[turn(zl, k), r], "Tzg", turn(zl, k) * 2 + r)
        for w in range(4):
            TO[c, x, r, :, w * piece : (w + 1) * piece] = TW[w, r]
        mine = TO.at[c, x, r]
        for k in KS:
            send(mine, mine, x_dev(turn(x, k)), "Tax", x * 2 + r)
        send(mine, mine, core, "Tac", 0)
    AMd[zh, y] = jnp.full((8, 128), jnp.max(jnp.abs(TO[c, x].astype(F32))), F32)
    for p in dp_group:
        send(AMd.at[zh, y], AMd.at[zh, y], p, "Md", zh * 4 + y)

    for k in KS:
        v = turn(x, k)
        arrive(HID.at[c, v], "Hx", v)
        send(HID.at[c, v], HID.at[c, v], core, "Hc", 0)
    for r in range(2):
        pass_on(TO, "Tax", "Tac", r)

    loads[4].wait()
    arrive(HID.at[oc], "Hc", 0)
    part = dot(HID[...].reshape(16 * ROWS, -1), wd[...]).reshape(SPf.shape)
    SPf[...] = part
    SPs[...] = part.astype(BF)
    for k in KS:
        v = turn(y, k)
        send(SPs.at[:, v], SPr.at[y], y_dev(v), "SPy", y)
    loads[3].wait()
    arrive(TO.at[oc], "Tac", 0)
    part = dot(TO[...].reshape(16 * ROWS, -1), dpj[...]).reshape(TPf.shape)
    TPf[...] = part
    TPs[...] = part.astype(BF)
    for k in KS:
        v = turn(y, k)
        send(TPs.at[:, v], TPr.at[y], y_dev(v), "TPy", y)

    for i in KS + (0,):
        for j in KS + (0,):
            if i or j:
                arrive(AMd.at[turn(zh, i), turn(y, j)], "Md", turn(zh, i) * 4 + turn(y, j))
    AMc[x, c] = jnp.max(AMd[...].reshape(16, 8, 128), axis=0)
    for p in pairs:
        send(AMc.at[x, c], AMc.at[x, c], p, "Mc", x * 2 + c)
    for k in KS:
        send(ABZ.at[zl], ABZ.at[zl], zl_dev(turn(zl, k)), "ABzl", zl)

    for k in KS:
        arrive(TPr.at[turn(y, k)], "TPy", turn(y, k))
        arrive(SPr.at[turn(y, k)], "SPy", turn(y, k))
    for k in KS:
        for b in range(2):
            arrive(AMc.at[turn(x, k), b], "Mc", turn(x, k) * 2 + b)
    arrive(AMc.at[x, oc], "Mc", x * 2 + oc)
    scale = (4.0 / jnp.max(AMc[...].reshape(8, 8, 128), axis=0))[0:1, 0:1]
    halves = (oc, c)
    for j, p in enumerate(halves):
        for i in range(2):
            z = 2 * p + i
            target, student = TPf[z, y], SPf[z, y]
            for k in KS:
                target = target + TPr[turn(y, k), z].astype(F32)
                student = student + SPr[turn(y, k), z].astype(F32)
            OZ[zh, z] = ((student - target * scale) * 0.5).astype(BF)
        part_of = OZ.at[zh, pl.ds(2 * p, 2)]
        for k in KS:
            send(part_of, part_of, zh_dev(turn(zh, k)), "Oz", zh * 2 + j)
    for k in KS:
        arrive(ABZ.at[turn(zl, k)], "ABzl", turn(zl, k))
    for a in range(2):
        for r in range(2):
            AB[c, x, a, r, :, 0:512] = ABZ[r, a]
            AB[c, x, a, r, :, 512:fs] = ABZ[2 + r, a][:, 512 - shift :]
    for k in KS:
        send(AB.at[c, x], AB.at[c, x], x_dev(turn(x, k)), "ABx", x)
    send(AB.at[c, x], AB.at[c, x], core, "ABc", 0)
    for j, p in enumerate(halves):
        for k in KS:
            arrive(OZ.at[turn(zh, k), pl.ds(2 * p, 2)], "Oz", turn(zh, k) * 2 + j)
        for i in range(2):
            z = 2 * p + i
            total = OZ[0, z].astype(F32)
            for w in range(1, 4):
                total = total + OZ[w, z].astype(F32)
            OG[z, y] = total.astype(BF)
        part_of = OG.at[pl.ds(2 * p, 2), y]
        for k in KS:
            send(part_of, part_of, y_dev(turn(y, k)), "Oy", y * 2 + j)

    for k in KS:
        v = turn(x, k)
        arrive(AB.at[c, v], "ABx", v)
        send(AB.at[c, v], AB.at[c, v], core, "ABc", 0)

    for k in KS:
        arrive(OG.at[pl.ds(2 * oc, 2), turn(y, k)], "Oy", turn(y, k) * 2)
    GCs[...] = dot_nt(OG[pl.ds(2 * oc, 2)].reshape(128, -1), wd[...]).astype(BF).reshape(GCs.shape)
    for r in range(2):
        send(GCs.at[:, r], GCr.at[:, r], core, "Gc", r)
    for k in KS:
        arrive(OG.at[pl.ds(2 * c, 2), turn(y, k)], "Oy", turn(y, k) * 2 + 1)
    GOWN[...] = dot_nt(OG[pl.ds(2 * c, 2)].reshape(128, -1), wd[...]).reshape(GOWN.shape)
    for r in range(2):
        scatter_x(GOWN, GCr, GXs, GXr, "Gc", "Gx", r)
    gd_o[...] = dot_tn(HID[...].reshape(16 * ROWS, -1), OG[...].reshape(16 * ROWS, -1)).astype(BF)
    store(gd_o, gd_h)
    for r in range(2):
        share_zl(GOWN, GCr, GXr, GZ, "Gx", "Gzl", r)
    arrive(AB.at[oc], "ABc", 0)
    for r in range(2):
        gather_x(GZ, HG, "Gzl", "Gax", "Gac", r)
    for r in range(2):
        pass_on(HG, "Gax", "Gac", r)
    arrive(HG.at[oc], "Gac", 0)
    for cc in range(2):
        for v in range(4):
            g = HG[cc, v].astype(F32)
            GG[cc, v] = (g * AB[cc, v, 0].astype(F32)).astype(BF)
            UG[cc, v] = (g * AB[cc, v, 1].astype(F32)).astype(BF)

    gates, ups = GG[...].reshape(16 * ROWS, -1), UG[...].reshape(16 * ROWS, -1)
    part = (dot_nt(gates, wg[...]) + dot_nt(ups, wu[...])).reshape(IPf.shape)
    IPf[...] = part
    IPs[...] = part.astype(BF)
    for i in KS + (0,):
        z = turn(zh, i)
        for k in KS:
            v = turn(y, k)
            send(IPs.at[z, v], IPr.at[y, z], y_dev(v), "Iy", y * 4 + z)
    gg_o[...] = dot(XT[...], gates).astype(BF)
    store(gg_o, gg_h)
    for i in KS + (0,):
        z = turn(zh, i)
        for k in KS:
            arrive(IPr.at[turn(y, k), z], "Iy", turn(y, k) * 4 + z)
        total = IPf[z, y]
        for k in KS:
            total = total + IPr[turn(y, k), z].astype(F32)
        if i:
            IZs[z] = total.astype(BF)
            send(IZs.at[z], IZr.at[zh], zh_dev(z), "Iz", zh)
    gu_o[...] = dot(XT[...], ups).astype(BF)
    store(gu_o, gu_h)
    for k in KS:
        arrive(IZr.at[turn(zh, k)], "Iz", turn(zh, k))
    for k in KS:
        total = total + IZr[turn(zh, k)].astype(F32)
    ig_o[...] = total.astype(BF)
    store(ig_o, ig_h)
    for copy in sent[-N_SEND:]:
        copy.wait_send()
    for copy in stores:
        copy.wait()


def hand_over(gg, gu, gd, ig, gg_o, gu_o, gd_o, ig_o, gg_v, gu_v, gd_v, ig_v, sem):
    ways = []
    for a, b, o in ((gg, gg_v, gg_o), (gu, gu_v, gu_o), (gd, gd_v, gd_o)):
        half = a.shape[0] // 2
        ways += [(a.at[pl.ds(i * half, half)], b.at[pl.ds(i * half, half)], o.at[pl.ds(i * half, half)]) for i in range(2)]
    loads = [pltpu.make_async_copy(a, b, sem.at[0, i]) for i, (a, b, _) in enumerate(ways)]
    stores = [pltpu.make_async_copy(b, o, sem.at[1, i]) for i, (_, b, o) in enumerate(ways)]
    last = pltpu.make_async_copy(ig, ig_v, sem.at[0, len(ways)])
    for load in loads + [last]:
        load.start()
    for load, store in zip(loads, stores):
        load.wait()
        store.start()
    last.wait()
    ig_o[...] = ig_v[...].astype(F32)[: ig_o.shape[0]].astype(BF)
    for store in stores:
        store.wait()


def body(
    teacher_hidden,
    teacher_down,
    scale_index,
    distill_proj,
    assignment,
    student_input,
    w_gate,
    w_up,
    w_down,
):
    tokens, ft = teacher_hidden.shape
    dt, ds = distill_proj.shape
    fs = w_gate.shape[1]

    def v(shape, dtype=BF):
        return pltpu.VMEM(shape, dtype)

    dp4 = (4, 4, ROWS)
    scratch = [
        pltpu.SMEM(scale_index.shape, jnp.int32), pltpu.SMEM(assignment.shape, jnp.int32), v((tokens, ft)), v((tokens, ds)),
        v((ds, fs)), v((ds, fs)), v((fs, ds)), v((ROWS, ds)),
        v((ft, dt)), v((dt, ds)), v((ds, fs)), v((ds, fs)), v((fs, ds)), v((16, ROWS, 16 * ROWS)), v(dp4 + (ft,)), v(dp4 + (ds,)), v((ds, 16 * ROWS)),
        v((2, 4, 32, fs), F32), v((2, 4, 32, fs), F32), v((2, 4, 32, fs), F32), v((4, 2, 32, fs)), v((4, 2, 32, fs)),
        v((4, 2, 16, 512), F32), v((4, 2, 16, 512)), v((4, 2, 16, 512)), v((4, 16, 512)), v((4, 2, 16, 512)),
        v((2, 4, 2, 16, fs)), v((2, 4, 2, 2, 16, fs)),
        v((4, 2, 16, dt), F32), v((4, 2, 16, dt), F32), v((4, 2, 16, dt), F32), v((4, 2, 16, dt), F32), v((4, 2, 16, dt), F32),
        v((4, 2, 16, dt // 4), F32), v((4, 2, 16, dt // 4), F32), v((4, 2, 16, dt // 4)), v((2, 4, 2, 16, dt)),
        v((4, 4, 8, 128), F32), v((4, 2, 8, 128), F32),
        v(dp4 + (ds,), F32), v(dp4 + (ds,)), v(dp4 + (ds,)), v(dp4 + (ds,), F32), v(dp4 + (ds,)), v(dp4 + (ds,)),
        v(dp4 + (ds,)), v(dp4 + (ds,)),
        v((4, 2, 16, fs)), v((4, 2, 16, fs)), v((4, 2, 16, fs), F32), v((4, 2, 16, fs)), v((4, 2, 16, fs)),
        v((4, 2, 16, fs)), v((2, 4, 2, 16, fs)), v((2, 4, 2, 16, fs)), v((2, 4, 2, 16, fs)),
        v(dp4 + (ds,), F32), v(dp4 + (ds,)), v(dp4 + (ds,)), v((4, ROWS, ds)), v((4, ROWS, ds)),
        pltpu.SemaphoreType.DMA((N_SEND,)), pltpu.SemaphoreType.DMA((N_RECV,)), pltpu.SemaphoreType.DMA((9,)), pltpu.SemaphoreType.DMA((4,)),
    ]
    vm, hbm = pl.BlockSpec(memory_space=pltpu.VMEM), pl.BlockSpec(memory_space=pl.ANY)
    sds = jax.ShapeDtypeStruct
    grad_gate, grad_up, grad_down, input_grad = pl.pallas_call(
        kernel,
        out_shape=(sds((ds, fs), BF), sds((ds, fs), BF), sds((fs, ds), BF), sds((ROWS, ds), BF)),
        in_specs=[hbm] * 9,
        out_specs=(hbm,) * 4,
        scratch_shapes=scratch,
        compiler_params=pltpu.CompilerParams(collective_id=0, has_side_effects=True, vmem_limit_bytes=56 << 20),
        name="distill_step",
    )(scale_index, assignment, teacher_hidden, student_input, teacher_down, distill_proj, w_gate, w_up, w_down)
    return pl.pallas_call(
        hand_over,
        out_shape=(sds((ds, fs), BF), sds((ds, fs), BF), sds((fs, ds), BF), sds((tokens, ds), BF)),
        in_specs=[hbm] * 4,
        out_specs=(hbm,) * 3 + (vm,),
        scratch_shapes=[v((ds, fs)), v((ds, fs)), v((fs, ds)), v((ROWS, ds)), pltpu.SemaphoreType.DMA((2, 7))],
        name="hand_over",
    )(grad_gate, grad_up, grad_down, input_grad)


def solution(mesh):
    placed = (
        P("dp", "mp"),
        P("mp", "dp"),
        P("mp"),
        P("dp", "mp"),
        P(),
        P("dp", "mp"),
        P("mp", "dp"),
        P("mp", "dp"),
        P("dp", "mp"),
    )
    return jax.shard_map(
        body,
        mesh=mesh,
        in_specs=placed,
        out_specs=(P("mp", "dp"), P("mp", "dp"), P("dp", "mp"), P("dp", "mp")),
        check_vma=False,
    )
```

time: 116 us -> 112 us (0.966)
  Pallas kernels: 115 us -> 111 us
    pallas_call x1, Pallas kernels: 112 us -> 108 us  [body(): pl.pallas_call(kernel, out_shape=(sds((ds, fs), BF), sds((ds, fs), BF), s...]
where the time goes in v3:
time: 112 us; the launch traced here: 111 us
  Pallas kernels  111 us (99%)
    pallas_call x1, Pallas kernels, body(): pl.pallas_call(kernel, out_shape=(sds((ds, fs), BF), sds((ds, fs), BF), s...  108 us
    pallas_call x1, Pallas kernels, body(): pl.pallas_call(hand_over, out_shape=(sds((ds, fs), BF), sds((ds, fs), BF)...  2.84 us

profile of v3, /device:TPU:1, one launch (start us, length us, event | category | flops | bytes accessed | tf_op | source)
XLA Modules:
  0.0 111.5 jit_solution(912973686976822093)
XLA Ops:
  0.6 108.0 %distill_step.1 = (bf16[256,896]{1,0:T(8,128)(2,1)}, bf16[256,896]{1,0:T(8,128)(2,1)}, bf16[896,256]{1,0:T(8,128)(2,1)}, bf16[16,256]{1,0:T(8,128)(2,1)}) custom-call(s32[13]{0:T(128)} %index_h.1, s32[224]{0:T(256)} %assign_h.1, bf16[14,832]{1,0:T(8,128)(2,1)} %th_h.1, bf16[14,256]{1,0:T(8,128)(2,1)} %xin_h.1, bf16[832,1024]{1,0:T(8,128)(2,1)} %td_h.1, ...), custom_call_target="tpu_custom_call" | custom-call | tf_op jit(solution)/shard_map/distill_step/pallas_call | solution.py:500
  108.6 2.8 %hand_over.1 = (bf16[256,896]{1,0:T(8,128)(2,1)}, bf16[256,896]{1,0:T(8,128)(2,1)}, bf16[896,256]{1,0:T(8,128)(2,1)}, bf16[14,256]{1,0:T(8,128)(2,1)}) custom-call(bf16[256,896]{1,0:T(8,128)(2,1)} %get-tuple-element.8.gg, bf16[256,896]{1,0:T(8,128)(2,1)} %get-tuple-element.9.gu, bf16[896,256]{1,0:T(8,128)(2,1)} %get-tuple-element.10.gd, ...), custom_call_target="tpu_custom_call" | custom-call | tf_op jit(solution)/shard_map/hand_over/pallas_call | solution.py:509

commit v4 on v3

--- a/solution.py
+++ b/solution.py
@@ -15,7 +15,7 @@
 RECV = {}
 N_RECV = 0
 for _name, _n in (
-    ("Sz", 4), ("Tz", 4), ("Sy", 4), ("Ty", 4), ("Sc", 2), ("Tc", 2), ("Sx", 8), ("Tx", 8), ("Szl", 8), ("Tzl", 8), ("Tzg", 8),
+    ("Sz", 4), ("Tz", 8), ("Sy", 4), ("Ty", 4), ("Sc", 2), ("Tc", 2), ("Sx", 8), ("Tx", 8), ("Szl", 8), ("Tzl", 8), ("Tzg", 8),
     ("Hzl", 4), ("ABzl", 4), ("Hx", 4), ("Hc", 1), ("ABx", 4), ("ABc", 1), ("Tax", 8), ("Tac", 1),
     ("Md", 16), ("Mc", 8), ("TPy", 4), ("SPy", 4), ("Iz", 4),
 ):
@@ -124,7 +124,7 @@
         partners += [x_dev(turn(x, k)), at(x=turn(x, k), c=oc), zl_dev(turn(zl, k))]
     dp_group = [at(zh=turn(zh, i), y=turn(y, j)) for i in KS + (0,) for j in KS + (0,)][:-1]
     pairs = [at(x=turn(x, k), c=b) for k in KS for b in (oc, c)] + [core]
-    partners += dp_group
+    partners = dp_group + partners
     for p in partners:
         pl.semaphore_signal(barrier, inc=1, device_id=p, device_id_type=MESH)
     loads = [
@@ -177,18 +177,24 @@
     lax.fori_loop(0, 16, place, 0)
     pl.semaphore_wait(barrier, len(partners))
 
-    for buf, nz, ny in ((XG, "Sz", "Sy"), (TG, "Tz", "Ty")):
-        own = buf.at[zh, y]
-        for k in KS:
-            send(own, own, zh_dev(turn(zh, k)), nz, zh)
-        for k in KS:
-            send(own, own, y_dev(turn(y, k)), ny, y)
-    for buf, nz, ny in ((XG, "Sz", "Sy"), (TG, "Tz", "Ty")):
+    def columns(buf, z, low, high):
+        return buf.at[z, y, :, pl.ds(low, high - low)]
+
+    parts = ((XG, "Sz", "Sy", 0, xin.shape[1], 0), (TG, "Tz", "Ty", 0, ft, 0))
+    for buf, nz, ny, low, high, slot in parts:
+        own = columns(buf, zh, low, high)
+        for k in KS:
+            send(own, own, zh_dev(turn(zh, k)), nz, zh + slot)
+    for buf, ny in ((XG, "Sy"), (TG, "Ty")):
+        for k in KS:
+            send(buf.at[zh, y], buf.at[zh, y], y_dev(turn(y, k)), ny, y)
+    for buf, nz, ny, low, high, slot in parts:
         for k in KS:
             z = turn(zh, k)
-            arrive(buf.at[z, y], nz, z)
+            block = columns(buf, z, low, high)
+            arrive(block, nz, z + slot)
             for j in KS:
-                send(buf.at[z, y], buf.at[z, y], y_dev(turn(y, j)), ny, y)
+                send(block, block, y_dev(turn(y, j)), ny, y)
 
     for j in KS:
         arrive(XG.at[:, turn(y, j)], "Sy", turn(y, j))
@@ -294,7 +300,7 @@
         for k in KS:
             send(mine, mine, x_dev(turn(x, k)), "Tax", x * 2 + r)
         send(mine, mine, core, "Tac", 0)
-    AMd[zh, y] = jnp.full((8, 128), jnp.max(jnp.abs(TO[c, x].astype(F32))), F32)
+    AMd[zh, y] = jnp.full((8, 128), jnp.max(jnp.abs(TW[...].astype(F32))), F32)
     for p in dp_group:
         send(AMd.at[zh, y], AMd.at[zh, y], p, "Md", zh * 4 + y)
 
@@ -302,25 +308,28 @@
         v = turn(x, k)
         arrive(HID.at[c, v], "Hx", v)
         send(HID.at[c, v], HID.at[c, v], core, "Hc", 0)
+    def product(rows, weights, full, rounded, half):
+        out = dot(rows[half].reshape(8 * ROWS, -1), weights[...]).reshape(2, 4, ROWS, -1)
+        full[pl.ds(2 * half, 2)] = out
+        rounded[pl.ds(2 * half, 2)] = out.astype(BF)
+
+    def spread(rounded, into, name):
+        for k in KS:
+            v = turn(y, k)
+            send(rounded.at[:, v], into.at[y], y_dev(v), name, y)
+
+    loads[4].wait()
+    product(HID, wd, SPf, SPs, c)
     for r in range(2):
         pass_on(TO, "Tax", "Tac", r)
-
-    loads[4].wait()
     arrive(HID.at[oc], "Hc", 0)
-    part = dot(HID[...].reshape(16 * ROWS, -1), wd[...]).reshape(SPf.shape)
-    SPf[...] = part
-    SPs[...] = part.astype(BF)
-    for k in KS:
-        v = turn(y, k)
-        send(SPs.at[:, v], SPr.at[y], y_dev(v), "SPy", y)
+    product(HID, wd, SPf, SPs, oc)
+    spread(SPs, SPr, "SPy")
     loads[3].wait()
+    product(TO, dpj, TPf, TPs, c)
     arrive(TO.at[oc], "Tac", 0)
-    part = dot(TO[...].reshape(16 * ROWS, -1), dpj[...]).reshape(TPf.shape)
-    TPf[...] = part
-    TPs[...] = part.astype(BF)
-    for k in KS:
-        v = turn(y, k)
-        send(TPs.at[:, v], TPr.at[y], y_dev(v), "TPy", y)
+    product(TO, dpj, TPf, TPs, oc)
+    spread(TPs, TPr, "TPy")
 
     for i in KS + (0,):
         for j in KS + (0,):
@@ -393,27 +402,31 @@
     store(gd_o, gd_h)
     for r in range(2):
         share_zl(GOWN, GCr, GXr, GZ, "Gx", "Gzl", r)
+    for r in range(2):
+        gather_x(GZ, HG, "Gzl", "Gax", "Gac", r)
+    for r in range(2):
+        pass_on(HG, "Gax", "Gac", r)
+
+    def input_part(half):
+        for v in range(4):
+            g = HG[half, v].astype(F32)
+            GG[half, v] = (g * AB[half, v, 0].astype(F32)).astype(BF)
+            UG[half, v] = (g * AB[half, v, 1].astype(F32)).astype(BF)
+        part = dot_nt(GG[half].reshape(8 * ROWS, -1), wg[...]) + dot_nt(UG[half].reshape(8 * ROWS, -1), wu[...])
+        part = part.reshape(2, 4, ROWS, -1)
+        IPf[pl.ds(2 * half, 2)] = part
+        IPs[pl.ds(2 * half, 2)] = part.astype(BF)
+        for i in range(2):
+            z = 2 * half + i
+            for k in KS:
+                v = turn(y, k)
+                send(IPs.at[z, v], IPr.at[y, z], y_dev(v), "Iy", y * 4 + z)
+
+    input_part(c)
     arrive(AB.at[oc], "ABc", 0)
-    for r in range(2):
-        gather_x(GZ, HG, "Gzl", "Gax", "Gac", r)
-    for r in range(2):
-        pass_on(HG, "Gax", "Gac", r)
     arrive(HG.at[oc], "Gac", 0)
-    for cc in range(2):
-        for v in range(4):
-            g = HG[cc, v].astype(F32)
-            GG[cc, v] = (g * AB[cc, v, 0].astype(F32)).astype(BF)
-            UG[cc, v] = (g * AB[cc, v, 1].astype(F32)).astype(BF)
-
+    input_part(oc)
     gates, ups = GG[...].reshape(16 * ROWS, -1), UG[...].reshape(16 * ROWS, -1)
-    part = (dot_nt(gates, wg[...]) + dot_nt(ups, wu[...])).reshape(IPf.shape)
-    IPf[...] = part
-    IPs[...] = part.astype(BF)
-    for i in KS + (0,):
-        z = turn(zh, i)
-        for k in KS:
-            v = turn(y, k)
-            send(IPs.at[z, v], IPr.at[y, z], y_dev(v), "Iy", y * 4 + z)
     gg_o[...] = dot(XT[...], gates).astype(BF)
     store(gg_o, gg_h)
     for i in KS + (0,):
@@ -443,8 +456,8 @@
 def hand_over(gg, gu, gd, ig, gg_o, gu_o, gd_o, ig_o, gg_v, gu_v, gd_v, ig_v, sem):
     ways = []
     for a, b, o in ((gg, gg_v, gg_o), (gu, gu_v, gu_o), (gd, gd_v, gd_o)):
-        half = a.shape[0] // 2
-        ways += [(a.at[pl.ds(i * half, half)], b.at[pl.ds(i * half, half)], o.at[pl.ds(i * half, half)]) for i in range(2)]
+        part = a.shape[0] // 2
+        ways += [tuple(r.at[pl.ds(i * part, part)] for r in (a, b, o)) for i in range(2)]
     loads = [pltpu.make_async_copy(a, b, sem.at[0, i]) for i, (a, b, _) in enumerate(ways)]
     stores = [pltpu.make_async_copy(b, o, sem.at[1, i]) for i, (_, b, o) in enumerate(ways)]
     last = pltpu.make_async_copy(ig, ig_v, sem.at[0, len(ways)])

time: 112 us -> 111 us (level)
  no operation moved by 1% of the time
where the time goes in v4:
time: 111 us
  Pallas kernels  110 us (99%)
    pallas_call x1, Pallas kernels, body(): pl.pallas_call(kernel, out_shape=(sds((ds, fs), BF), sds((ds, fs), BF), s...  107 us
    pallas_call x1, Pallas kernels, body(): pl.pallas_call(hand_over, out_shape=(sds((ds, fs), BF), sds((ds, fs), BF)...  2.84 us

profile of v4, /device:TPU:1, one launch (start us, length us, event | category | flops | bytes accessed | tf_op | source)
XLA Modules:
  0.0 110.9 jit_solution(2423770699244878193)
XLA Ops:
  0.6 107.4 %distill_step.1 = (bf16[256,896]{1,0:T(8,128)(2,1)}, bf16[256,896]{1,0:T(8,128)(2,1)}, bf16[896,256]{1,0:T(8,128)(2,1)}, bf16[16,256]{1,0:T(8,128)(2,1)}) custom-call(s32[13]{0:T(128)} %index_h.1, s32[224]{0:T(256)} %assign_h.1, bf16[14,832]{1,0:T(8,128)(2,1)} %th_h.1, bf16[14,256]{1,0:T(8,128)(2,1)} %xin_h.1, bf16[832,1024]{1,0:T(8,128)(2,1)} %td_h.1, ...), custom_call_target="tpu_custom_call" | custom-call | tf_op jit(solution)/shard_map/distill_step/pallas_call | solution.py:513
  108.0 2.8 %hand_over.1 = (bf16[256,896]{1,0:T(8,128)(2,1)}, bf16[256,896]{1,0:T(8,128)(2,1)}, bf16[896,256]{1,0:T(8,128)(2,1)}, bf16[14,256]{1,0:T(8,128)(2,1)}) custom-call(bf16[256,896]{1,0:T(8,128)(2,1)} %get-tuple-element.8.gg, bf16[256,896]{1,0:T(8,128)(2,1)} %get-tuple-element.9.gu, bf16[896,256]{1,0:T(8,128)(2,1)} %get-tuple-element.10.gd, ...), custom_call_target="tpu_custom_call" | custom-call | tf_op jit(solution)/shard_map/hand_over/pallas_call | solution.py:522

commit v5 on v4

--- a/solution.py
+++ b/solution.py
@@ -294,15 +294,16 @@
     for r in range(2):
         for k in KS:
             arrive(TW.at[turn(zl, k), r], "Tzg", turn(zl, k) * 2 + r)
+    AMd[zh, y] = jnp.full((8, 128), jnp.max(jnp.abs(TW[...].astype(F32))), F32)
+    for p in dp_group:
+        send(AMd.at[zh, y], AMd.at[zh, y], p, "Md", zh * 4 + y)
+    for r in range(2):
         for w in range(4):
             TO[c, x, r, :, w * piece : (w + 1) * piece] = TW[w, r]
         mine = TO.at[c, x, r]
         for k in KS:
             send(mine, mine, x_dev(turn(x, k)), "Tax", x * 2 + r)
         send(mine, mine, core, "Tac", 0)
-    AMd[zh, y] = jnp.full((8, 128), jnp.max(jnp.abs(TW[...].astype(F32))), F32)
-    for p in dp_group:
-        send(AMd.at[zh, y], AMd.at[zh, y], p, "Md", zh * 4 + y)
 
     for k in KS:
         v = turn(x, k)

time: 111 us -> 111 us (level)
  no operation moved by 1% of the time
where the time goes in v5:
time: 111 us
  Pallas kernels  110 us (99%)
    pallas_call x1, Pallas kernels, body(): pl.pallas_call(kernel, out_shape=(sds((ds, fs), BF), sds((ds, fs), BF), s...  108 us
    pallas_call x1, Pallas kernels, body(): pl.pallas_call(hand_over, out_shape=(sds((ds, fs), BF), sds((ds, fs), BF)...  2.84 us

profile of v5, /device:TPU:1, one launch (start us, length us, event | category | flops | bytes accessed | tf_op | source)
XLA Modules:
  0.0 111.0 jit_solution(6391733397364462354)
XLA Ops:
  0.6 107.5 %distill_step.1 = (bf16[256,896]{1,0:T(8,128)(2,1)}, bf16[256,896]{1,0:T(8,128)(2,1)}, bf16[896,256]{1,0:T(8,128)(2,1)}, bf16[16,256]{1,0:T(8,128)(2,1)}) custom-call(s32[13]{0:T(128)} %index_h.1, s32[224]{0:T(256)} %assign_h.1, bf16[14,832]{1,0:T(8,128)(2,1)} %th_h.1, bf16[14,256]{1,0:T(8,128)(2,1)} %xin_h.1, bf16[832,1024]{1,0:T(8,128)(2,1)} %td_h.1, ...), custom_call_target="tpu_custom_call" | custom-call | tf_op jit(solution)/shard_map/distill_step/pallas_call | solution.py:514
  108.2 2.8 %hand_over.1 = (bf16[256,896]{1,0:T(8,128)(2,1)}, bf16[256,896]{1,0:T(8,128)(2,1)}, bf16[896,256]{1,0:T(8,128)(2,1)}, bf16[14,256]{1,0:T(8,128)(2,1)}) custom-call(bf16[256,896]{1,0:T(8,128)(2,1)} %get-tuple-element.8.gg, bf16[256,896]{1,0:T(8,128)(2,1)} %get-tuple-element.9.gu, bf16[896,256]{1,0:T(8,128)(2,1)} %get-tuple-element.10.gd, ...), custom_call_target="tpu_custom_call" | custom-call | tf_op jit(solution)/shard_map/hand_over/pallas_call | solution.py:523
